TPU v7x, 32 devices: a whole 2x2x4 slice. The times are simulated.
32 devices in a mesh: ctx: 8 (over y, x, core), head: 4 (over z).
Axes of the slice: x: 2, y: 2, z: 4, core: 2. Of those that a mesh axis runs over, the one named last changes fastest.
Arguments:
- inputs: bfloat16 [4096, 4096], P('ctx'), may hold values from -8 to 8
- query_weight: bfloat16 [4096, 2048], P(None, 'head'), may hold values from -0.09375 to 0.09375
- key_weight: bfloat16 [4096, 512], P(None, 'head'), may hold values from -0.09375 to 0.09375
- value_weight: bfloat16 [4096, 512], P(None, 'head'), may hold values from -0.09375 to 0.09375
- out_grad: bfloat16 [4096, 2048], P('ctx', 'head'), may hold values from -6 to 6
- doc_lengths: int32 [8], replicated, may hold values from 128 to 1536, as said below
Outputs:
- attn_out: bfloat16 [4096, 2048], P('ctx', 'head')
- input_grad: bfloat16 [4096, 4096], P('ctx', 'head')
- query_weight_grad: float32 [4096, 2048], P('ctx', 'head')
- key_weight_grad: float32 [4096, 512], P('ctx', 'head')
- value_weight_grad: float32 [4096, 512], P('ctx', 'head')
Inputs may be any that keep to these rules, and one draw needn't show every extreme that they name: `doc_lengths`: each length is a positive multiple of 128; the lengths sum to 4096; the largest is exactly 1536.
All inputs are finite; a program needn't handle non-finite values.
Results may differ from a plain program's by a relative error of at most 0.018.
The roundings to bfloat16 on the way count: a program that leaves them out, or rounds other values in their place, can miss the bound.
Values may be sent and summed in bfloat16 or wider, within the bound.
No kernel may reach another device: no remote copies, remote signals or barrier semaphores. Data moves between devices by JAX's collectives and lax.ppermute only.
A program may use at most 128 MiB of HBM per device.

v0:
```python
from functools import partial

import jax
import jax.numpy as jnp
from jax import lax
from jax.experimental import pallas as pl
from jax.experimental.pallas import tpu as pltpu
from jax.sharding import PartitionSpec as P

HD = 128
GROUP = 4
SPAN = 3
GRAIN = 128
TILE = 256
CHUNK = 512
MIB = 2**20

NEG = -1e30
LOG2E = 1.4426950408889634


def dot_nt(left_mat, right_mat):
    return lax.dot_general(
        left_mat, right_mat, (((1,), (1,)), ((), ())), preferred_element_type=jnp.float32
    )


def dot_tn(left_mat, right_mat):
    return lax.dot_general(
        left_mat, right_mat, (((0,), (0,)), ((), ())), preferred_element_type=jnp.float32
    )


def dot_nn(left_mat, right_mat):
    return jnp.dot(left_mat, right_mat, preferred_element_type=jnp.float32)


def in_hbm(*arrays):
    return [pltpu.with_memory_space_constraint(array, pltpu.HBM) for array in arrays]


def cut_kernel(*refs):
    weight_refs, piece_refs, sems = refs[:3], refs[3:-1], refs[-1]
    head, ctx = lax.axis_index("head"), lax.axis_index("ctx")
    n_head = len(piece_refs) + 1
    piece = piece_refs[0].shape[0]
    copies = []
    for distance, piece_ref in enumerate(piece_refs, 1):
        group = lax.rem(head + distance, n_head)
        first = group * (weight_refs[0].shape[0] // n_head) + ctx * piece
        at = 0
        for number, weight_ref in enumerate(weight_refs):
            cols = weight_ref.shape[1]
            copies.append(
                pltpu.make_async_copy(
                    weight_ref.at[pl.ds(pl.multiple_of(first, piece), piece), :],
                    piece_ref.at[:, pl.ds(at, cols)],
                    sems.at[distance - 1, number],
                )
            )
            at += cols
    for copy in copies:
        copy.start()
    for copy in copies:
        copy.wait()


def cut_rows(weights, n_head, piece):
    cols = sum(weight.shape[1] for weight in weights)
    anywhere = pl.BlockSpec(memory_space=pl.ANY)
    return pl.pallas_call(
        cut_kernel,
        out_shape=(jax.ShapeDtypeStruct((piece, cols), jnp.bfloat16),) * (n_head - 1),
        in_specs=[anywhere] * 3,
        out_specs=(pl.BlockSpec(memory_space=pltpu.VMEM),) * (n_head - 1),
        scratch_shapes=[pltpu.SemaphoreType.DMA((n_head - 1, 3))],
        cost_estimate=pl.CostEstimate(flops=0, bytes_accessed=2 * MIB, transcendentals=0),
        name="cut_rows",
    )(*in_hbm(*weights))


def project_kernel(x_ref, *refs):
    n = len(refs) - 4
    weight_refs, (out_ref, x_here, weight_here, sems) = refs[:n], refs[n:]
    rows = x_ref.shape[0]
    chunks = []
    for step in range(x_ref.shape[1] // CHUNK):
        part = pl.ds(step * CHUNK, CHUNK)
        copies = [pltpu.make_async_copy(x_ref.at[:, part], x_here.at[:, part], sems.at[step, 0])]
        at = 0
        for number, weight_ref in enumerate(weight_refs):
            cols = pl.ds(at, weight_ref.shape[1])
            at += weight_ref.shape[1]
            copies.append(
                pltpu.make_async_copy(
                    weight_ref.at[part, :], weight_here.at[part, cols], sems.at[step, 1 + number]
                )
            )
        for copy in copies:
            copy.start()
        chunks.append((part, copies))
    total = jnp.zeros((rows, weight_here.shape[1]), jnp.float32)
    for part, copies in chunks:
        for copy in copies:
            copy.wait()
        total = total + dot_nn(x_here[:, part], weight_here[part, :])
    out_ref[...] = total.astype(out_ref.dtype)


def project(inputs, weights, name):
    rows, width = inputs.shape
    cols = sum(weight.shape[1] for weight in weights)
    anywhere = pl.BlockSpec(memory_space=pl.ANY)
    return pl.pallas_call(
        project_kernel,
        in_specs=[anywhere] * (len(weights) + 1),
        out_specs=pl.BlockSpec(memory_space=pltpu.VMEM),
        out_shape=jax.ShapeDtypeStruct((rows, cols), jnp.bfloat16),
        scratch_shapes=[
            pltpu.VMEM((rows, width), jnp.bfloat16),
            pltpu.VMEM((width, cols), jnp.bfloat16),
            pltpu.SemaphoreType.DMA((width // CHUNK, len(weights) + 1)),
        ],
        compiler_params=pltpu.CompilerParams(vmem_limit_bytes=24 * MIB),
        cost_estimate=pl.CostEstimate(
            flops=2 * rows * width * cols, bytes_accessed=2 * width * (rows + cols), transcendentals=0
        ),
        name=name,
    )(*in_hbm(inputs, *weights))


def merge_kernel(d2_ref, bundle_ref, out_ref):
    rows, cols = out_ref.shape
    core = lax.axis_index("ctx") % 2
    here = pl.ds(bundle_ref.shape[0] - rows, rows)
    near, far = bundle_ref[here, :cols], bundle_ref[here, cols:]
    other = jnp.where(core == 1, near.astype(jnp.float32), far.astype(jnp.float32))
    out_ref[...] = (d2_ref[...].astype(jnp.float32) + other).astype(out_ref.dtype)


def combine_kernel(own_ref, merged_ref, far_ref, bundle_ref, low_ref, turned_ref):
    rows, cols = own_ref.shape
    core = lax.axis_index("ctx") % 2
    near = bundle_ref[bundle_ref.shape[0] - rows :, :cols].astype(jnp.float32)
    total = own_ref[...] + merged_ref[...].astype(jnp.float32) + far_ref[...].astype(jnp.float32)
    total = total + jnp.where(core == 0, near, 0.0)
    low_ref[...] = total.astype(jnp.bfloat16)
    turned_ref[...] = total.T.astype(jnp.bfloat16)


def small_kernel(kernel, shapes, name, *operands):
    def whole(shape):
        return pl.BlockSpec(shape, lambda i: (0, 0))

    return pl.pallas_call(
        kernel,
        grid=(1,),
        out_shape=tuple(jax.ShapeDtypeStruct(shape, dtype) for shape, dtype in shapes),
        in_specs=[whole(operand.shape) for operand in operands],
        out_specs=tuple(whole(shape) for shape, dtype in shapes),
        compiler_params=pltpu.CompilerParams(vmem_limit_bytes=20 * MIB),
        cost_estimate=pl.CostEstimate(flops=4 * MIB, bytes_accessed=4 * MIB, transcendentals=0),
        name=name,
    )(*operands)


def terms_kernel(chips, turned_ref, other_turned_ref, x_ref, other_x_ref, *refs):
    out_refs, (x_here, sum_here, low_here, in_sems, out_sems) = refs[:chips], refs[chips:]
    cols, kept = out_refs[0].shape
    ctx = lax.axis_index("ctx")
    order = [*range(1, chips), 0]
    coming = {}
    for chip in order:
        first = pl.multiple_of((((ctx // 2) ^ chip) * 2 + ctx % 2) * kept, kept)
        coming[chip] = [
            pltpu.make_async_copy(ref.at[:, pl.ds(first, kept)], x_here.at[chip, side], in_sems.at[chip, side])
            for side, ref in enumerate((x_ref, other_x_ref))
        ]
        for copy in coming[chip]:
            copy.start()
    going = []
    for chip in order:
        for copy in coming[chip]:
            copy.wait()
        term = dot_nn(turned_ref[:cols, :], x_here[chip, 0]) + dot_nn(other_turned_ref[:cols, :], x_here[chip, 1])
        here = sum_here if chip == 0 else low_here.at[chip]
        here[...] = term.astype(here.dtype)
        copy = pltpu.make_async_copy(here, out_refs[chip], out_sems.at[chip])
        copy.start()
        going.append(copy)
    for copy in going:
        copy.wait()


def weight_terms(turned, other_turned, cols, inputs, other_inputs, n_ctx, name):
    rows = turned.shape[1]
    kept = inputs.shape[1] // n_ctx
    chips = n_ctx // 2
    vmem = pl.BlockSpec(memory_space=pltpu.VMEM)
    anywhere = pl.BlockSpec(memory_space=pl.ANY)
    return pl.pallas_call(
        partial(terms_kernel, chips),
        in_specs=[vmem, vmem, anywhere, anywhere],
        out_specs=(anywhere,) * chips,
        out_shape=tuple(
            jax.ShapeDtypeStruct((cols, kept), jnp.float32 if chip == 0 else jnp.bfloat16)
            for chip in range(chips)
        ),
        scratch_shapes=[
            pltpu.VMEM((chips, 2, rows, kept), jnp.bfloat16),
            pltpu.VMEM((cols, kept), jnp.float32),
            pltpu.VMEM((chips, cols, kept), jnp.bfloat16),
            pltpu.SemaphoreType.DMA((chips, 2)),
            pltpu.SemaphoreType.DMA((chips,)),
        ],
        compiler_params=pltpu.CompilerParams(vmem_limit_bytes=24 * MIB),
        cost_estimate=pl.CostEstimate(
            flops=4 * cols * rows * kept * chips, bytes_accessed=10 * MIB, transcendentals=0
        ),
        name=name,
    )(turned, other_turned, inputs, other_inputs)


def rows_kernel(n_in, *refs):
    in_refs, out_refs = refs[:n_in], refs[n_in:]
    total = in_refs[0][...]
    for in_ref in in_refs[1:]:
        total = total + in_ref[...].astype(jnp.float32)
    at = 0
    for out_ref in out_refs:
        cols = slice(at, at + out_ref.shape[1])
        at = cols.stop
        out_ref[...] = total[cols, :].T


def weight_rows(terms, widths, name):
    kept = terms[0].shape[1]
    shapes = [((kept, width), jnp.float32) for width in widths]
    return small_kernel(partial(rows_kernel, len(terms)), shapes, name, *terms)


def products_kernel(count, has_base, *refs):
    left_refs, rows_refs, out_ref = refs[:count], refs[count : 2 * count], refs[-1]
    total = refs[2 * count][...] if has_base else None
    for left_ref, rows_ref in zip(left_refs, rows_refs):
        rows = rows_ref[...]
        term = dot_nt(left_ref[...], rows.reshape(-1, rows.shape[-1]))
        total = term if total is None else total + term
    out_ref[...] = total.astype(out_ref.dtype)


def products(pairs, base, out_width, n_head, dtype, name):
    rows = base.shape[0] if base is not None else pairs[0][0][0].shape[0]
    block = 512
    n_blocks = out_width // block
    left_specs, right_specs, lefts, rights = [], [], [], []
    flops = 0
    for (left, *place), right in pairs:
        lefts.append(left)
        if len(place) == 2:
            column, cols = place
            left_specs.append(pl.BlockSpec((rows, cols), partial(lambda column, i: (0, column), column)))
        else:
            cols = left.shape[1]
            left_specs.append(
                pl.BlockSpec(
                    (rows, cols),
                    partial(
                        lambda steps, i: ((lax.axis_index("head") + n_head - steps) % n_head, 0), place[0]
                    ),
                )
            )
        flops += 2 * rows * cols * out_width
        if isinstance(right, tuple):
            gathered, steps, first = right
            piece = gathered.shape[2]
            rights.append(gathered)
            right_specs.append(
                pl.BlockSpec(
                    (block // piece, 1, piece, cols),
                    partial(lambda step, at, i: (i, step, 0, at), steps - 1, first // cols),
                )
            )
        else:
            rights.append(right)
            right_specs.append(
                pl.BlockSpec((block, cols), lambda i: (lax.axis_index("head") * n_blocks + i, 0))
            )
    part = pl.BlockSpec((rows, block), lambda i: (0, i))
    extra = [] if base is None else [base]
    return pl.pallas_call(
        partial(products_kernel, len(pairs), base is not None),
        grid=(n_blocks,),
        in_specs=left_specs + right_specs + [part] * len(extra),
        out_specs=part,
        out_shape=jax.ShapeDtypeStruct((rows, out_width), dtype),
        compiler_params=pltpu.CompilerParams(vmem_limit_bytes=20 * MIB),
        cost_estimate=pl.CostEstimate(flops=flops, bytes_accessed=8 * MIB, transcendentals=0),
        name=name,
    )(*lefts, *in_hbm(*rights), *extra)


def attention_kernel(
    first_ref, query_ref, grad_ref, kv0, kv1, kv2, kv3,
    out_ref, dq_ref, bundle_ref, d0, d2, d3,
    kv_ref, acc_ref, score_ref, sum_ref, sems,
):
    rows = query_ref.shape[0]
    copies = [
        pltpu.make_async_copy(block, kv_ref.at[pl.ds(slot * rows, rows), :], sems.at[slot])
        for slot, block in enumerate((kv3, kv2, kv1, kv0))
    ]
    for copy in copies:
        copy.start()
    acc_ref[...] = jnp.zeros_like(acc_ref)
    for copy in copies:
        copy.wait()
    factor = HD ** (-0.5)
    wide = GROUP * GRAIN
    streams = range(TILE // GRAIN)
    key_local = lax.broadcasted_iota(jnp.int32, (TILE, wide), 0)
    query_local = lax.broadcasted_iota(jnp.int32, (TILE, wide), 1) % GRAIN
    heads = [slice(h * HD, (h + 1) * HD) for h in range(GROUP)]

    def tile_rows(tile):
        return pl.ds(pl.multiple_of(tile * TILE, TILE), TILE)

    for pair in range(rows // TILE):
        places = [pl.ds(pair * TILE + g * GRAIN, GRAIN) for g in streams]
        query = [jnp.concatenate([query_ref[here, cols] for cols in heads], axis=0) for here in places]
        grad = [jnp.concatenate([grad_ref[here, cols] for cols in heads], axis=0) for here in places]
        first = [first_ref[pair * len(places) + g] for g in streams]
        last = (SPAN * rows) // TILE + pair
        low = first[0] // TILE
        sum_ref[...] = jnp.zeros_like(sum_ref)

        def score_tile(tile, carry, diagonal):
            here = tile_rows(tile)
            following = []
            for g in streams:
                top, total = carry[g]
                score = dot_nt(kv_ref[here, :HD], query[g]) * (factor * LOG2E)
                keep = key_local >= first[g] - tile * TILE
                if diagonal:
                    keep = keep & (key_local <= query_local + g * GRAIN)
                score = jnp.where(keep, score, NEG)
                score_ref[g, here, :] = score
                new_top = jnp.maximum(top, jnp.max(score, axis=0, keepdims=True))
                weight = jnp.sum(jnp.exp2(score - new_top), axis=0, keepdims=True)
                following.append((new_top, total * jnp.exp2(top - new_top) + weight))
            return tuple(following)

        state = tuple(
            (jnp.full((1, wide), NEG, jnp.float32), jnp.zeros((1, wide), jnp.float32)) for g in streams
        )
        state = lax.fori_loop(low, last, lambda tile, carry: score_tile(tile, carry, False), state)
        state = score_tile(last, state, True)
        lse = [top + jnp.log2(total) for top, total in state]

        def output_tile(tile, carry):
            here = tile_rows(tile)
            value_grad = acc_ref[here, HD:]
            for g in streams:
                prob = jnp.exp2(score_ref[g, here, :] - lse[g])
                score_ref[g, here, :] = prob
                prob = prob.astype(jnp.bfloat16)
                sum_ref[g] += dot_tn(kv_ref[here, HD:], prob)
                value_grad = value_grad + dot_nn(prob, grad[g])
            acc_ref[here, HD:] = value_grad
            return carry

        lax.fori_loop(low, last + 1, output_tile, 0)
        delta = []
        for g in streams:
            turned = sum_ref[g].astype(jnp.bfloat16).astype(jnp.float32)
            delta.append(
                jnp.sum(turned * grad[g].astype(jnp.float32).T, axis=0, keepdims=True)
            )
            out_rows = turned.T.astype(jnp.bfloat16)
            for head, cols in enumerate(heads):
                out_ref[places[g], cols] = out_rows[head * GRAIN : (head + 1) * GRAIN]
        sum_ref[...] = jnp.zeros_like(sum_ref)

        def gradient_tile(tile, carry):
            here = tile_rows(tile)
            key_grad = acc_ref[here, :HD]
            for g in streams:
                dprob = dot_nt(kv_ref[here, HD:], grad[g])
                dscore = (score_ref[g, here, :] * (dprob - delta[g])).astype(jnp.bfloat16)
                key_grad = key_grad + dot_nn(dscore, query[g])
                sum_ref[g] += dot_tn(kv_ref[here, :HD], dscore)
            acc_ref[here, :HD] = key_grad
            return carry

        lax.fori_loop(low, last + 1, gradient_tile, 0)
        for g in streams:
            turned = sum_ref[g] * factor
            dquery = turned.T.astype(jnp.bfloat16)
            for head, cols in enumerate(heads):
                part = slice(head * GRAIN, (head + 1) * GRAIN)
                dq_ref[places[g], cols] = dquery[part]
                bundle_ref[cols, places[g]] = turned[:, part].astype(jnp.bfloat16)
    cols = query_ref.shape[1]
    for distance, blocks in enumerate(
        ((d0,), (bundle_ref.at[cols:, : 2 * HD],), (d2,), (d3, bundle_ref.at[cols:, 2 * HD :]))
    ):
        place = pl.ds((SPAN - distance) * rows, rows)
        key_grad, value_grad = acc_ref[place, :HD] * factor, acc_ref[place, HD:]
        for block in blocks:
            block[:, :HD] = key_grad.astype(block.dtype)
            block[:, HD:] = value_grad.astype(block.dtype)


def attention(first, query, grad, kv_list):
    rows, cols = query.shape
    window = (SPAN + 1) * rows
    low = jax.ShapeDtypeStruct((rows, cols), jnp.bfloat16)
    bundle = jax.ShapeDtypeStruct((cols + rows, rows), jnp.bfloat16)
    own = jax.ShapeDtypeStruct((rows, 2 * HD), jnp.float32)
    sent = jax.ShapeDtypeStruct((rows, 2 * HD), jnp.bfloat16)
    vmem = pl.BlockSpec(memory_space=pltpu.VMEM)
    anywhere = pl.BlockSpec(memory_space=pl.ANY)
    return pl.pallas_call(
        attention_kernel,
        out_shape=(low, low, bundle, own, sent, sent),
        in_specs=[pl.BlockSpec(memory_space=pltpu.SMEM), vmem, vmem] + [anywhere] * (SPAN + 1),
        out_specs=(vmem,) * 6,
        scratch_shapes=[
            pltpu.VMEM((window, 2 * HD), jnp.bfloat16),
            pltpu.VMEM((window, 2 * HD), jnp.float32),
            pltpu.VMEM((TILE // GRAIN, window, GROUP * GRAIN), jnp.float32),
            pltpu.VMEM((TILE // GRAIN, HD, GROUP * GRAIN), jnp.float32),
            pltpu.SemaphoreType.DMA((SPAN + 1,)),
        ],
        compiler_params=pltpu.CompilerParams(vmem_limit_bytes=24 * MIB),
        cost_estimate=pl.CostEstimate(
            flops=6 * 2 * rows * window * cols, bytes_accessed=6 * MIB, transcendentals=0
        ),
        name="attention",
    )(first, query, grad, *kv_list)


def shift(value, axis, steps):
    count = lax.axis_size(axis)
    pairs = [(i, i + steps) for i in range(count) if 0 <= i + steps < count]
    return lax.ppermute(value, axis, pairs)


def swap(value, axis, mask):
    return lax.ppermute(value, axis, [(i, i ^ mask) for i in range(lax.axis_size(axis))])


def rotate(value, axis, steps):
    count = lax.axis_size(axis)
    return lax.ppermute(value, axis, [(i, (i + steps) % count) for i in range(count)])


def body(inputs, query_weight, key_weight, value_weight, out_grad, doc_lengths):
    tok_rows, width = inputs.shape
    n_ctx = lax.axis_size("ctx")
    n_head = lax.axis_size("head")
    chips = n_ctx // 2
    ctx = lax.axis_index("ctx")
    head = lax.axis_index("head")
    q_cols = query_weight.shape[1]
    k_cols = key_weight.shape[1]

    weights = (query_weight, key_weight, value_weight)
    out_width = width // n_head
    piece = out_width // n_ctx
    pieces = cut_rows(weights, n_head, piece)
    pieces, inputs = lax.optimization_barrier((pieces, inputs))
    pieces = [rotate(rows, "head", step) for step, rows in enumerate(pieces, 1)]

    kv_loc = project(inputs, (key_weight, value_weight), "project_kv")
    kv_list = [kv_loc] + [shift(kv_loc, "ctx", distance) for distance in range(1, SPAN + 1)]
    late_inputs, kv_loc = lax.optimization_barrier((inputs, kv_loc))
    query = project(late_inputs, (query_weight,), "project_query")
    query, kv_list, pieces, inputs = lax.optimization_barrier((query, kv_list, pieces, inputs))
    gathered = lax.all_gather(jnp.concatenate(pieces, axis=0), "ctx", axis=0, tiled=True)
    gathered = gathered.reshape(n_ctx, n_head - 1, piece, q_cols + 2 * k_cols)

    other_inputs = swap(inputs, "ctx", 1)

    granules = tok_rows // GRAIN
    window_start = (ctx - SPAN) * tok_rows
    positions = ctx * tok_rows + GRAIN * jnp.arange(granules, dtype=jnp.int32)
    doc_ends = jnp.cumsum(doc_lengths)
    starts = jnp.sum(
        jnp.where(doc_ends[None, :] <= positions[:, None], doc_lengths[None, :], 0), axis=1
    )
    attn_out, dq_low, bundle, own_grads, mid_grads, far_grads = attention(
        starts - window_start, query, out_grad, kv_list
    )

    other_bundle = swap(bundle, "ctx", 1)
    dq_up = rotate(dq_low, "head", 1)
    dq_down = rotate(dq_low, "head", -1)
    far = lax.ppermute(
        far_grads, "ctx", [(source, source - SPAN) for source in range(0, n_ctx, 2) if source >= SPAN]
    )
    kv_shape = (tok_rows, 2 * k_cols)
    merged, = small_kernel(merge_kernel, [(kv_shape, jnp.bfloat16)], "merge", mid_grads, other_bundle)
    merged = shift(merged, "ctx", -2)

    q_terms = weight_terms(bundle, other_bundle, q_cols, inputs, other_inputs, n_ctx, "query_terms")
    q_moved = [swap(q_terms[chips - 1], "ctx", 2 * (chips - 1))]
    far, merged, dq_up, dq_down, dq_low, q_moved, q_terms = lax.optimization_barrier(
        (far, merged, dq_up, dq_down, dq_low, q_moved, q_terms)
    )
    dkv_low, dkv_turned = small_kernel(
        combine_kernel, [(kv_shape, jnp.bfloat16), (kv_shape[::-1], jnp.bfloat16)], "combine",
        own_grads, merged, far, other_bundle,
    )
    dkv_all = lax.all_gather(dkv_low, "head", axis=0, tiled=True)
    dq_far = rotate(dq_up, "head", 1)
    other_dkv = swap(dkv_turned, "ctx", 1)
    q_moved += [swap(q_terms[chip], "ctx", 2 * chip) for chip in range(1, chips - 1)]
    kv_terms = weight_terms(
        dkv_turned, other_dkv, 2 * k_cols, inputs, other_inputs, n_ctx, "key_terms"
    )
    kv_moved = [swap(term, "ctx", 2 * chip) for chip, term in enumerate(kv_terms) if chip > 0]
    _, dq_low, dq_up, dq_down = lax.optimization_barrier((kv_terms, dq_low, dq_up, dq_down))

    grad_sum = products(
        (
            ((dq_low, 0, q_cols), query_weight),
            ((dq_up, 0, q_cols), (gathered, 1, 0)),
            ((dq_down, 0, q_cols), (gathered, 3, 0)),
        ),
        None, out_width, n_head, jnp.float32, "products_near",
    )
    grad_sum, q_moved, kv_moved = lax.optimization_barrier((grad_sum, q_moved, kv_moved))
    q_grad, = weight_rows([q_terms[0], *q_moved], (q_cols,), "query_rows")
    k_grad, v_grad = weight_rows([kv_terms[0], *kv_moved], (k_cols, k_cols), "key_rows")
    q_grad, k_grad, v_grad, grad_sum = lax.optimization_barrier((q_grad, k_grad, v_grad, grad_sum))
    input_grad = products(
        (
            ((dq_far, 0, q_cols), (gathered, 2, 0)),
            ((dkv_low, 0, k_cols), key_weight),
            ((dkv_low, 1, k_cols), value_weight),
            *(((dkv_all, step), (gathered, step, q_cols)) for step in range(1, n_head)),
        ),
        grad_sum, out_width, n_head, jnp.bfloat16, "products_far",
    )
    return (attn_out, input_grad, q_grad, k_grad, v_grad)


def solution(mesh):
    return jax.shard_map(
        body,
        mesh=mesh,
        in_specs=(
            P("ctx", None),
            P(None, "head"),
            P(None, "head"),
            P(None, "head"),
            P("ctx", "head"),
            P(),
        ),
        out_specs=(P("ctx", "head"),) * 5,
        check_vma=False,
    )
```

profile of v0, /device:TPU:0, one launch (start us, length us, event | category | flops | bytes accessed | tf_op | source)
XLA Modules:
  0.0 146.7 jit_solution(7552999710477400332)
XLA Ops:
  7.2 2.0 %cut_rows.1 = (bf16[128,768]{1,0:T(8,128)(2,1)}, bf16[128,768]{1,0:T(8,128)(2,1)}, bf16[128,768]{1,0:T(8,128)(2,1)}) custom-call(bf16[4096,512]{1,0:T(8,128)(2,1)} %refs_3_.1, bf16[4096,128]{1,0:T(8,128)(2,1)} %refs_7_.1, bf16[4096,128]{1,0:T(8,128)(2,1)} %refs_8_.1), custom_call_target="tpu_custom_call" | custom-call | bytes 2097152 | tf_op jit(solution)/shard_map/cut_rows/pallas_call | solution.py:71
  9.3 3.1 %collective-permute-start.3 = (bf16[128,768]{1,0:T(8,128)(2,1)}, bf16[128,768]{1,0:T(8,128)(2,1)S(1)}, u32[]{:S(2)}, u32[]{:S(2)}) collective-permute-start(bf16[128,768]{1,0:T(8,128)(2,1)} %get-tuple-element.68), channel_id=1, source_target_pairs={{0,1},{1,2},{2,3},{3,0},{4,5},{5,6},{6,7},{7,4},{8,9},{9,10},{10,1... | collective-permute-start | bytes 589832 | tf_op jit(solution)/shard_map/ppermute | solution.py:455
  12.3 4.2 %project_kv.1.kv0 = bf16[512,256]{1,0:T(8,128)(2,1)S(1)} custom-call(bf16[512,4096]{1,0:T(8,128)(2,1)} %x_ref.3, bf16[4096,128]{1,0:T(8,128)(2,1)} %refs_7_.1, bf16[4096,128]{1,0:T(8,128)(2,1)} %refs_8_.1), custom_call_target="tpu_custom_call" | custom-call | flops 1073741824 | bytes 6291456 | tf_op jit(solution)/shard_map/project_kv/pallas_call | solution.py:114
  16.6 1.6 %collective-permute-start = (bf16[512,256]{1,0:T(8,128)(2,1)S(1)}, bf16[512,256]{1,0:T(8,128)(2,1)S(1)}, u32[]{:S(2)}, u32[]{:S(2)}) collective-permute-start(bf16[512,256]{1,0:T(8,128)(2,1)S(1)} %project_kv.1.kv0), channel_id=1, source_target_pairs={{0,4},{4,8},{8,12},{12,16},{16,20},{20,24},{24,28},{1,5},{5,9},{9,... | collective-permute-start | bytes 786440 | tf_op jit(solution)/shard_map/ppermute | solution.py:446
  18.2 3.9 %collective-permute-start.1 = (bf16[512,256]{1,0:T(8,128)(2,1)S(1)}, bf16[512,256]{1,0:T(8,128)(2,1)S(1)}, u32[]{:S(2)}, u32[]{:S(2)}) collective-permute-start(bf16[512,256]{1,0:T(8,128)(2,1)S(1)} %project_kv.1.kv0), channel_id=1, source_target_pairs={{0,8},{4,12},{8,16},{12,20},{16,24},{20,28},{1,9},{5,13},{9,17},{1... | collective-permute-start | bytes 786440 | tf_op jit(solution)/shard_map/ppermute | solution.py:446
  22.1 4.3 %collective-permute-start.2 = (bf16[512,256]{1,0:T(8,128)(2,1)S(1)}, bf16[512,256]{1,0:T(8,128)(2,1)S(1)}, u32[]{:S(2)}, u32[]{:S(2)}) collective-permute-start(bf16[512,256]{1,0:T(8,128)(2,1)S(1)} %project_kv.1.kv0), channel_id=1, source_target_pairs={{0,12},{4,16},{8,20},{12,24},{16,28},{1,13},{5,17},{9,21},{13,25},... | collective-permute-start | bytes 786440 | tf_op jit(solution)/shard_map/ppermute | solution.py:446
  26.4 2.7 %collective-permute-start.4 = (bf16[128,768]{1,0:T(8,128)(2,1)S(1)}, bf16[128,768]{1,0:T(8,128)(2,1)S(1)}, u32[]{:S(2)}, u32[]{:S(2)}) collective-permute-start(bf16[128,768]{1,0:T(8,128)(2,1)S(1)} %copy-done.16), channel_id=1, source_target_pairs={{0,2},{1,3},{2,0},{3,1},{4,6},{5,7},{6,4},{7,5},{8,10},{9,11},{10,... | collective-permute-start | bytes 589832 | tf_op jit(solution)/shard_map/ppermute | solution.py:455
  29.1 1.3 collective-permute-start.5
  30.4 4.3 %project_query.1.query_ref = bf16[512,512]{1,0:T(8,128)(2,1)S(1)} custom-call(bf16[512,4096]{1,0:T(8,128)(2,1)} %x_ref.3, bf16[4096,512]{1,0:T(8,128)(2,1)} %refs_3_.1), custom_call_target="tpu_custom_call" | custom-call | flops 2147483648 | bytes 8388608 | tf_op jit(solution)/shard_map/project_query/pallas_call | solution.py:114
  34.7 4.1 %collective-permute-done.4 = bf16[128,768]{1,0:T(8,128)(2,1)S(1)} collective-permute-done((bf16[128,768]{1,0:T(8,128)(2,1)S(1)}, bf16[128,768]{1,0:T(8,128)(2,1)S(1)}, u32[]{:S(2)}, u32[]{:S(2)}) %collective-permute-start.4) | collective-permute-done | bytes 196640 | tf_op jit(solution)/shard_map/ppermute | solution.py:455
  40.2 7.1 %attention.1 = (bf16[512,512]{1,0:T(8,128)(2,1)}, bf16[512,512]{1,0:T(8,128)(2,1)S(1)}, bf16[1024,512]{1,0:T(8,128)(2,1)S(1)}, f32[512,256]{1,0:T(8,128)S(1)}, b...) custom-call(s32[4]{0:T(128)S(1)} %broadcast_subtract_fusion.first_ref, ...), custom_call_target="tpu_custom_call" | custom-call | flops 6442450944 | bytes 6291456 | tf_op jit(solution)/shard_map/attention/pallas_call | solution.py:423
  47.3 6.8 %collective-permute-start.7 = (bf16[1024,512]{1,0:T(8,128)(2,1)S(1)}, bf16[1024,512]{1,0:T(8,128)(2,1)S(1)}, u32[]{:S(2)}, u32[]{:S(2)}) collective-permute-start(bf16[1024,512]{1,0:T(8,128)(2,1)S(1)} %get-tuple-element.79.turned_ref), channel_id=1, source_target_pairs={{0,4},{4,0},{8,12},{12,8},{16,20},{20,16},{24,28},{28,24},{1,5},{5... | collective-permute-start | bytes 3145736 | tf_op jit(solution)/shard_map/ppermute | solution.py:450
  54.2 5.3 %collective-permute-start.10 = (bf16[512,512]{1,0:T(8,128)(2,1)S(1)}, bf16[512,512]{1,0:T(8,128)(2,1)S(1)}, u32[]{:S(2)}, u32[]{:S(2)}) collective-permute-start(bf16[512,512]{1,0:T(8,128)(2,1)S(1)} %get-tuple-element.102.refs_0_), channel_id=1, source_target_pairs={{0,3},{1,0},{2,1},{3,2},{4,7},{5,4},{6,5},{7,6},{8,11},{9,8},{10,9... | collective-permute-start | bytes 1572872 | tf_op jit(solution)/shard_map/ppermute | solution.py:455
  59.5 4.2 %query_terms.1 = (f32[512,512]{1,0:T(8,128)S(1)}, bf16[512,512]{1,0:T(8,128)(2,1)S(1)}, bf16[512,512]{1,0:T(8,128)(2,1)}, bf16[512,512]{1,0:T(8,128)(2,1)S(1)}) custom-call(bf16[1024,512]{1,0:T(8,128)(2,1)S(1)} %get-tuple-element.79.turned_ref, bf16[1024,512]{1,0:T(8,128)(2,1)S(1)} %collective-permute-done.7.bundle_ref.other_turned_ref, ...), custom_call_target="tpu_custom_call" | custom-call | flops 2147483648 | bytes 10485760 | tf_op jit(solution)/shard_map/query_terms/pallas_call | solution.py:201
  64.6 1.3 collective-permute-start.8
  65.9 5.9 %collective-permute-done.10.refs_2_ = bf16[512,512]{1,0:T(8,128)(2,1)S(1)} collective-permute-done((bf16[512,512]{1,0:T(8,128)(2,1)S(1)}, bf16[512,512]{1,0:T(8,128)(2,1)S(1)}, u32[]{:S(2)}, u32[]{:S(2)}) %collective-permute-start.10) | collective-permute-done | bytes 524320 | tf_op jit(solution)/shard_map/ppermute | solution.py:455
  71.8 11.2 %collective-permute-done.9.refs_1_ = bf16[512,512]{1,0:T(8,128)(2,1)} collective-permute-done((bf16[512,512]{1,0:T(8,128)(2,1)S(1)}, bf16[512,512]{1,0:T(8,128)(2,1)}, u32[]{:S(2)}, u32[]{:S(2)}) %collective-permute-start.9) | collective-permute-done | bytes 524320 | tf_op jit(solution)/shard_map/ppermute | solution.py:455
  83.0 12.6 %collective-permute-done.8.merged_ref = bf16[512,256]{1,0:T(8,128)(2,1)S(1)} collective-permute-done((bf16[512,256]{1,0:T(8,128)(2,1)S(1)}, bf16[512,256]{1,0:T(8,128)(2,1)S(1)}, u32[]{:S(2)}, u32[]{:S(2)}) %collective-permute-start.8) | collective-permute-done | bytes 262176 | tf_op jit(solution)/shard_map/ppermute | solution.py:446
  96.4 1.6 %collective-permute-start.15 = (bf16[512,512]{1,0:T(8,128)(2,1)S(1)}, bf16[512,512]{1,0:T(8,128)(2,1)S(1)}, u32[]{:S(2)}, u32[]{:S(2)}) collective-permute-start(bf16[512,512]{1,0:T(8,128)(2,1)S(1)} %get-tuple-element.106), channel_id=1, source_target_pairs={{0,8},{4,12},{8,0},{12,4},{16,24},{20,28},{24,16},{28,20},{1,9},{5... | collective-permute-start | bytes 1572872 | tf_op jit(solution)/shard_map/ppermute | solution.py:450
  98.0 2.6 %collective-permute-start.14 = (bf16[256,512]{1,0:T(8,128)(2,1)S(1)}, bf16[256,512]{1,0:T(8,128)(2,1)S(1)}, u32[]{:S(2)}, u32[]{:S(2)}) collective-permute-start(bf16[256,512]{1,0:T(8,128)(2,1)S(1)} %get-tuple-element.95.turned_ref), channel_id=1, source_target_pairs={{0,4},{4,0},{8,12},{12,8},{16,20},{20,16},{24,28},{28,24},{1,5},{5... | collective-permute-start | bytes 786440 | tf_op jit(solution)/shard_map/ppermute | solution.py:450
  100.7 1.7 %collective-permute-start.13 = (bf16[512,512]{1,0:T(8,128)(2,1)}, bf16[512,512]{1,0:T(8,128)(2,1)}, u32[]{:S(2)}, u32[]{:S(2)}) collective-permute-start(bf16[512,512]{1,0:T(8,128)(2,1)} %collective-permute-done.9.refs_1_), channel_id=1, source_target_pairs={{0,1},{1,2},{2,3},{3,0},{4,5},{5,6},{6,7},{7,4},{8,9},{9,10},{10,1... | collective-permute-start | bytes 1572872 | tf_op jit(solution)/shard_map/ppermute | solution.py:455
  102.4 2.2 %copy-done.1 = bf16[512,4096]{1,0:T(8,128)(2,1)S(1)} copy-done((bf16[512,4096]{1,0:T(8,128)(2,1)S(1)}, bf16[512,4096]{1,0:T(8,128)(2,1)}, u32[]{:S(2)}) %copy-start.1) | copy-done | bytes 4194328
  104.6 3.3 %key_terms.1 = (f32[256,512]{1,0:T(8,128)S(1)}, bf16[256,512]{1,0:T(8,128)(2,1)}, bf16[256,512]{1,0:T(8,128)(2,1)}, bf16[256,512]{1,0:T(8,128)(2,1)}) custom-call(bf16[256,512]{1,0:T(8,128)(2,1)S(1)} %get-tuple-element.95.turned_ref, bf16[256,512]{1,0:T(8,128)(2,1)S(1)} %collective-permute-done.14.other_turned_ref, bf16[512,4096]{1,0:T(8,128)(2,1)S(1)} %copy-done.1, ...), custom_call_target="tpu_custom_call" | custom-call | flops 1073741824 | bytes 10485760 | tf_op jit(solution)/shard_map/key_terms/pallas_call | solution.py:201
  109.0 2.0 %collective-permute-start.18 = (bf16[256,512]{1,0:T(8,128)(2,1)}, bf16[256,512]{1,0:T(8,128)(2,1)}, u32[]{:S(2)}, u32[]{:S(2)}) collective-permute-start(bf16[256,512]{1,0:T(8,128)(2,1)} %get-tuple-element.98), channel_id=1, source_target_pairs={{0,16},{4,20},{8,24},{12,28},{16,0},{20,4},{24,8},{28,12},{1,17},{... | collective-permute-start | bytes 786440 | tf_op jit(solution)/shard_map/ppermute | solution.py:450
  111.9 1.1 collective-permute-start.19
  115.1 3.9 %products_near.1.refs_12_ = f32[512,1024]{1,0:T(8,128)S(1)} custom-call(bf16[512,512]{1,0:T(8,128)(2,1)S(1)} %copy-done.4, bf16[512,512]{1,0:T(8,128)(2,1)} %collective-permute-done.9.refs_1_, bf16[512,512]{1,0:T(8,128)(2,1)S(1)} %copy-done.8, bf16[4096,512]{1,0:T(8,128)(2,1)} %refs_3_.1, bf16[8,3,128,768]{3,2,1,0:T(8,128)(2,1)} %bitcast.3, ...), custom_call_target="tpu_custom_call" | custom-call | flops 1610612736 | bytes 8388608 | tf_op jit(solution)/shard_map/products_near/pallas_call | solution.py:291
  119.0 7.1 %collective-permute-done.18.refs_2_ = bf16[256,512]{1,0:T(8,128)(2,1)} collective-permute-done((bf16[256,512]{1,0:T(8,128)(2,1)}, bf16[256,512]{1,0:T(8,128)(2,1)}, u32[]{:S(2)}, u32[]{:S(2)}) %collective-permute-start.18) | collective-permute-done | bytes 262176 | tf_op jit(solution)/shard_map/ppermute | solution.py:450
  126.1 2.0 %key_rows.1 = (f32[512,128]{1,0:T(8,128)}, f32[512,128]{1,0:T(8,128)}) custom-call(f32[256,512]{1,0:T(8,128)S(1)} %copy-done.12, bf16[256,512]{1,0:T(8,128)(2,1)S(1)} %collective-permute-done.17.refs_1_, bf16[256,512]{1,0:T(8,128)(2,1)} %collective-permute-done.18.refs_2_, bf16[256,512]{1,0:T(8,128)(2,1)} %collective-permute-done.19.refs_3_), custom_call_target="tpu_custom_call" | custom-call | flops 4194304 | bytes 4194304 | tf_op jit(solution)/shard_map/key_rows/pallas_call | solution.py:155
  128.0 2.4 %query_rows.1 = f32[512,512]{1,0:T(8,128)} custom-call(f32[512,512]{1,0:T(8,128)S(1)} %get-tuple-element.94.refs_0_, bf16[512,512]{1,0:T(8,128)(2,1)S(1)} %copy-done.6, bf16[512,512]{1,0:T(8,128)(2,1)S(1)} %copy-done.10, bf16[512,512]{1,0:T(8,128)(2,1)} %collective-permute-done.16.refs_3_), custom_call_target="tpu_custom_call" | custom-call | flops 4194304 | bytes 4194304 | tf_op jit(solution)/shard_map/query_rows/pallas_call | solution.py:155
  130.4 3.5 %all-gather.3.cloned.1.call-done.refs_3_.refs_4_.refs_5_ = bf16[2048,256]{1,0:T(8,128)(2,1)} async-done(((bf16[512,256]{1,0:T(8,128)(2,1)}), bf16[2048,256]{1,0:T(8,128)(2,1)}) %all-gather.3.cloned.1.call-update) | async-done | bytes 1048592 | tf_op jit(solution)/shard_map/all_gather | solution.py:515
  133.9 1.2 copy-done.2
  135.1 4.8 %products_far.1 = bf16[512,1024]{1,0:T(8,128)(2,1)} custom-call(bf16[512,512]{1,0:T(8,128)(2,1)} %collective-permute-done.13.refs_0_, bf16[512,256]{1,0:T(8,128)(2,1)} %get-tuple-element.90.refs_1_.refs_2_, bf16[512,256]{1,0:T(8,128)(2,1)} %get-tuple-element.90.refs_1_.refs_2_, bf16[2048,256]{1,0:T(8,128)(2,1)S(1)} %copy-done.2, ...), custom_call_target="tpu_custom_call" | custom-call | flops 1610612736 | bytes 8388608 | tf_op jit(solution)/shard_map/products_far/pallas_call | solution.py:291
  (65 shorter events, 7.3 us)
Async XLA Ops:
  7.2 105.8 %all-gather.5.cloned.1.call-start = ((), (), s32[]{:S(2)}) async-start(), calls=%async_computation.1 | async-start | bytes 5308416 | tf_op jit(solution)/shard_map/all_gather | solution.py:480
  9.2 17.2 %copy-start.16 = (bf16[128,768]{1,0:T(8,128)(2,1)S(1)}, bf16[128,768]{1,0:T(8,128)(2,1)}, u32[]{:S(2)}) copy-start(bf16[128,768]{1,0:T(8,128)(2,1)} %get-tuple-element.69) | copy-start | bytes 589828
  9.2 19.8 %copy-start.15 = (bf16[128,768]{1,0:T(8,128)(2,1)S(1)}, bf16[128,768]{1,0:T(8,128)(2,1)}, u32[]{:S(2)}) copy-start(bf16[128,768]{1,0:T(8,128)(2,1)} %get-tuple-element.70) | copy-start | bytes 589828
  9.3 19.8 %collective-permute-start.3 = (bf16[128,768]{1,0:T(8,128)(2,1)}, bf16[128,768]{1,0:T(8,128)(2,1)S(1)}, u32[]{:S(2)}, u32[]{:S(2)}) collective-permute-start(bf16[128,768]{1,0:T(8,128)(2,1)} %get-tuple-element.68), channel_id=1, source_target_pairs={{0,1},{1,2},{2,3},{3,0},{4,5},{5,6},{6,7},{7,4},{8,9},{9,10},{10,1... | collective-permute-start | bytes 589832 | tf_op jit(solution)/shard_map/ppermute | solution.py:455
  16.6 23.3 %copy-start.14 = (s32[8]{0:T(128)S(1)}, s32[8]{0:T(128)}, u32[]{:S(2)}) copy-start(s32[8]{0:T(128)} %param.11) | copy-start | bytes 100
  16.6 23.6 %copy-start.13 = (bf16[512,512]{1,0:T(8,128)(2,1)S(1)}, bf16[512,512]{1,0:T(8,128)(2,1)}, u32[]{:S(2)}) copy-start(bf16[512,512]{1,0:T(8,128)(2,1)} %grad_ref.1) | copy-start | bytes 1572868
  16.6 22.2 %collective-permute-start = (bf16[512,256]{1,0:T(8,128)(2,1)S(1)}, bf16[512,256]{1,0:T(8,128)(2,1)S(1)}, u32[]{:S(2)}, u32[]{:S(2)}) collective-permute-start(bf16[512,256]{1,0:T(8,128)(2,1)S(1)} %project_kv.1.kv0), channel_id=1, source_target_pairs={{0,4},{4,8},{8,12},{12,16},{16,20},{20,24},{24,28},{1,5},{5,9},{9,... | collective-permute-start | bytes 786440 | tf_op jit(solution)/shard_map/ppermute | solution.py:446
  18.2 20.6 %collective-permute-start.1 = (bf16[512,256]{1,0:T(8,128)(2,1)S(1)}, bf16[512,256]{1,0:T(8,128)(2,1)S(1)}, u32[]{:S(2)}, u32[]{:S(2)}) collective-permute-start(bf16[512,256]{1,0:T(8,128)(2,1)S(1)} %project_kv.1.kv0), channel_id=1, source_target_pairs={{0,8},{4,12},{8,16},{12,20},{16,24},{20,28},{1,9},{5,13},{9,17},{1... | collective-permute-start | bytes 786440 | tf_op jit(solution)/shard_map/ppermute | solution.py:446
  22.1 16.7 %collective-permute-start.2 = (bf16[512,256]{1,0:T(8,128)(2,1)S(1)}, bf16[512,256]{1,0:T(8,128)(2,1)S(1)}, u32[]{:S(2)}, u32[]{:S(2)}) collective-permute-start(bf16[512,256]{1,0:T(8,128)(2,1)S(1)} %project_kv.1.kv0), channel_id=1, source_target_pairs={{0,12},{4,16},{8,20},{12,24},{16,28},{1,13},{5,17},{9,21},{13,25},... | collective-permute-start | bytes 786440 | tf_op jit(solution)/shard_map/ppermute | solution.py:446
  26.4 12.4 %collective-permute-start.4 = (bf16[128,768]{1,0:T(8,128)(2,1)S(1)}, bf16[128,768]{1,0:T(8,128)(2,1)S(1)}, u32[]{:S(2)}, u32[]{:S(2)}) collective-permute-start(bf16[128,768]{1,0:T(8,128)(2,1)S(1)} %copy-done.16), channel_id=1, source_target_pairs={{0,2},{1,3},{2,0},{3,1},{4,6},{5,7},{6,4},{7,5},{8,10},{9,11},{10,... | collective-permute-start | bytes 589832 | tf_op jit(solution)/shard_map/ppermute | solution.py:455
  29.1 9.7 %collective-permute-start.5 = (bf16[128,768]{1,0:T(8,128)(2,1)S(1)}, bf16[128,768]{1,0:T(8,128)(2,1)S(1)}, u32[]{:S(2)}, u32[]{:S(2)}) collective-permute-start(bf16[128,768]{1,0:T(8,128)(2,1)S(1)} %copy-done.15), channel_id=1, source_target_pairs={{0,3},{1,0},{2,1},{3,2},{4,7},{5,4},{6,5},{7,6},{8,11},{9,8},{10,9... | collective-permute-start | bytes 589832 | tf_op jit(solution)/shard_map/ppermute | solution.py:455
  39.7 94.2 %all-gather.3.cloned.1.call-start = ((), (), s32[]{:S(2)}) async-start(), calls=%async_computation | async-start | bytes 1310720 | tf_op jit(solution)/shard_map/all_gather | solution.py:515
  39.7 19.7 %collective-permute-start.11 = (bf16[512,4096]{1,0:T(8,128)(2,1)}, bf16[512,4096]{1,0:T(8,128)(2,1)}, u32[]{:S(2)}, u32[]{:S(2)}) collective-permute-start(bf16[512,4096]{1,0:T(8,128)(2,1)} %x_ref.3), channel_id=1, source_target_pairs={{0,4},{4,0},{8,12},{12,8},{16,20},{20,16},{24,28},{28,24},{1,5},{5... | collective-permute-start | bytes 12582920 | tf_op jit(solution)/shard_map/ppermute | solution.py:450
  40.2 19.3 %copy-start = (bf16[512,4096]{1,0:T(8,128)(2,1)S(1)}, bf16[512,4096]{1,0:T(8,128)(2,1)}, u32[]{:S(2)}) copy-start(bf16[512,4096]{1,0:T(8,128)(2,1)} %x_ref.3) | copy-start | bytes 12582916
  47.3 16.4 %copy-start.3 = (bf16[512,512]{1,0:T(8,128)(2,1)}, bf16[512,512]{1,0:T(8,128)(2,1)S(1)}, u32[]{:S(2)}) copy-start(bf16[512,512]{1,0:T(8,128)(2,1)S(1)} %get-tuple-element.102.refs_0_) | copy-start | bytes 1572868
  47.3 12.1 %collective-permute-start.7 = (bf16[1024,512]{1,0:T(8,128)(2,1)S(1)}, bf16[1024,512]{1,0:T(8,128)(2,1)S(1)}, u32[]{:S(2)}, u32[]{:S(2)}) collective-permute-start(bf16[1024,512]{1,0:T(8,128)(2,1)S(1)} %get-tuple-element.79.turned_ref), channel_id=1, source_target_pairs={{0,4},{4,0},{8,12},{12,8},{16,20},{20,16},{24,28},{28,24},{1,5},{5... | collective-permute-start | bytes 3145736 | tf_op jit(solution)/shard_map/ppermute | solution.py:450
  54.2 17.6 %collective-permute-start.10 = (bf16[512,512]{1,0:T(8,128)(2,1)S(1)}, bf16[512,512]{1,0:T(8,128)(2,1)S(1)}, u32[]{:S(2)}, u32[]{:S(2)}) collective-permute-start(bf16[512,512]{1,0:T(8,128)(2,1)S(1)} %get-tuple-element.102.refs_0_), channel_id=1, source_target_pairs={{0,3},{1,0},{2,1},{3,2},{4,7},{5,4},{6,5},{7,6},{8,11},{9,8},{10,9... | collective-permute-start | bytes 1572872 | tf_op jit(solution)/shard_map/ppermute | solution.py:455
  59.5 23.5 %collective-permute-start.9 = (bf16[512,512]{1,0:T(8,128)(2,1)S(1)}, bf16[512,512]{1,0:T(8,128)(2,1)}, u32[]{:S(2)}, u32[]{:S(2)}) collective-permute-start(bf16[512,512]{1,0:T(8,128)(2,1)S(1)} %get-tuple-element.102.refs_0_), channel_id=1, source_target_pairs={{0,1},{1,2},{2,3},{3,0},{4,5},{5,6},{6,7},{7,4},{8,9},{9,10},{10,1... | collective-permute-start | bytes 1572872 | tf_op jit(solution)/shard_map/ppermute | solution.py:455
  63.8 31.8 %collective-permute-start.12 = (bf16[512,512]{1,0:T(8,128)(2,1)S(1)}, bf16[512,512]{1,0:T(8,128)(2,1)S(1)}, u32[]{:S(2)}, u32[]{:S(2)}) collective-permute-start(bf16[512,512]{1,0:T(8,128)(2,1)S(1)} %get-tuple-element.82), channel_id=1, source_target_pairs={{0,24},{4,28},{8,16},{12,20},{16,8},{20,12},{24,0},{28,4},{1,25},{... | collective-permute-start | bytes 1572872 | tf_op jit(solution)/shard_map/ppermute | solution.py:450
  63.8 2.1 %collective-permute-start.6 = (bf16[512,256]{1,0:T(8,128)(2,1)S(1)}, bf16[512,256]{1,0:T(8,128)(2,1)S(1)}, u32[]{:S(2)}, u32[]{:S(2)}) collective-permute-start(bf16[512,256]{1,0:T(8,128)(2,1)S(1)} %get-tuple-element.77), channel_id=1, source_target_pairs={{16,4},{24,12},{17,5},{25,13},{18,6},{26,14},{19,7},{27,15}} | collective-permute-start | bytes 786440 | tf_op jit(solution)/shard_map/ppermute | solution.py:499
  64.6 30.9 %collective-permute-start.8 = (bf16[512,256]{1,0:T(8,128)(2,1)S(1)}, bf16[512,256]{1,0:T(8,128)(2,1)S(1)}, u32[]{:S(2)}, u32[]{:S(2)}) collective-permute-start(bf16[512,256]{1,0:T(8,128)(2,1)S(1)} %merge.1), channel_id=1, source_target_pairs={{8,0},{12,4},{16,8},{20,12},{24,16},{28,20},{9,1},{13,5},{17,9},{2... | collective-permute-start | bytes 786440 | tf_op jit(solution)/shard_map/ppermute | solution.py:446
  71.8 24.6 %copy-start.7 = (bf16[512,512]{1,0:T(8,128)(2,1)}, bf16[512,512]{1,0:T(8,128)(2,1)S(1)}, u32[]{:S(2)}) copy-start(bf16[512,512]{1,0:T(8,128)(2,1)S(1)} %collective-permute-done.10.refs_2_) | copy-start | bytes 1572868
  96.4 14.6 %collective-permute-start.15 = (bf16[512,512]{1,0:T(8,128)(2,1)S(1)}, bf16[512,512]{1,0:T(8,128)(2,1)S(1)}, u32[]{:S(2)}, u32[]{:S(2)}) collective-permute-start(bf16[512,512]{1,0:T(8,128)(2,1)S(1)} %get-tuple-element.106), channel_id=1, source_target_pairs={{0,8},{4,12},{8,0},{12,4},{16,24},{20,28},{24,16},{28,20},{1,9},{5... | collective-permute-start | bytes 1572872 | tf_op jit(solution)/shard_map/ppermute | solution.py:450
  98.0 4.4 %collective-permute-start.14 = (bf16[256,512]{1,0:T(8,128)(2,1)S(1)}, bf16[256,512]{1,0:T(8,128)(2,1)S(1)}, u32[]{:S(2)}, u32[]{:S(2)}) collective-permute-start(bf16[256,512]{1,0:T(8,128)(2,1)S(1)} %get-tuple-element.95.turned_ref), channel_id=1, source_target_pairs={{0,4},{4,0},{8,12},{12,8},{16,20},{20,16},{24,28},{28,24},{1,5},{5... | collective-permute-start | bytes 786440 | tf_op jit(solution)/shard_map/ppermute | solution.py:450
  100.7 18.2 %collective-permute-start.16 = (bf16[512,512]{1,0:T(8,128)(2,1)}, bf16[512,512]{1,0:T(8,128)(2,1)}, u32[]{:S(2)}, u32[]{:S(2)}) collective-permute-start(bf16[512,512]{1,0:T(8,128)(2,1)} %get-tuple-element.107), channel_id=1, source_target_pairs={{0,16},{4,20},{8,24},{12,28},{16,0},{20,4},{24,8},{28,12},{1,17},{... | collective-permute-start | bytes 1572872 | tf_op jit(solution)/shard_map/ppermute | solution.py:450
  100.7 29.7 %collective-permute-start.13 = (bf16[512,512]{1,0:T(8,128)(2,1)}, bf16[512,512]{1,0:T(8,128)(2,1)}, u32[]{:S(2)}, u32[]{:S(2)}) collective-permute-start(bf16[512,512]{1,0:T(8,128)(2,1)} %collective-permute-done.9.refs_1_), channel_id=1, source_target_pairs={{0,1},{1,2},{2,3},{3,0},{4,5},{5,6},{6,7},{7,4},{8,9},{9,10},{10,1... | collective-permute-start | bytes 1572872 | tf_op jit(solution)/shard_map/ppermute | solution.py:455
  108.6 10.3 %collective-permute-start.17 = (bf16[256,512]{1,0:T(8,128)(2,1)}, bf16[256,512]{1,0:T(8,128)(2,1)S(1)}, u32[]{:S(2)}, u32[]{:S(2)}) collective-permute-start(bf16[256,512]{1,0:T(8,128)(2,1)} %get-tuple-element.97), channel_id=1, source_target_pairs={{0,8},{4,12},{8,0},{12,4},{16,24},{20,28},{24,16},{28,20},{1,9},{5... | collective-permute-start | bytes 786440 | tf_op jit(solution)/shard_map/ppermute | solution.py:450
  109.0 17.1 %collective-permute-start.18 = (bf16[256,512]{1,0:T(8,128)(2,1)}, bf16[256,512]{1,0:T(8,128)(2,1)}, u32[]{:S(2)}, u32[]{:S(2)}) collective-permute-start(bf16[256,512]{1,0:T(8,128)(2,1)} %get-tuple-element.98), channel_id=1, source_target_pairs={{0,16},{4,20},{8,24},{12,28},{16,0},{20,4},{24,8},{28,12},{1,17},{... | collective-permute-start | bytes 786440 | tf_op jit(solution)/shard_map/ppermute | solution.py:450
  111.9 14.2 %collective-permute-start.19 = (bf16[256,512]{1,0:T(8,128)(2,1)}, bf16[256,512]{1,0:T(8,128)(2,1)}, u32[]{:S(2)}, u32[]{:S(2)}) collective-permute-start(bf16[256,512]{1,0:T(8,128)(2,1)} %get-tuple-element.99), channel_id=1, source_target_pairs={{0,24},{4,28},{8,16},{12,20},{16,8},{20,12},{24,0},{28,4},{1,25},{... | collective-permute-start | bytes 786440 | tf_op jit(solution)/shard_map/ppermute | solution.py:450
  115.1 11.0 %copy-start.12 = (f32[256,512]{1,0:T(8,128)S(1)}, f32[256,512]{1,0:T(8,128)}, u32[]{:S(2)}) copy-start(f32[256,512]{1,0:T(8,128)} %copy-done.11) | copy-start | bytes 1572868
  115.1 13.0 %copy-start.6 = (bf16[512,512]{1,0:T(8,128)(2,1)S(1)}, bf16[512,512]{1,0:T(8,128)(2,1)}, u32[]{:S(2)}) copy-start(bf16[512,512]{1,0:T(8,128)(2,1)} %copy-done.5) | copy-start | bytes 1572868
  115.1 13.0 %copy-start.10 = (bf16[512,512]{1,0:T(8,128)(2,1)S(1)}, bf16[512,512]{1,0:T(8,128)(2,1)}, u32[]{:S(2)}) copy-start(bf16[512,512]{1,0:T(8,128)(2,1)} %copy-done.9) | copy-start | bytes 1572868
  (7 other events, 8.0 us)
Sparse Core Ops, SparseCore 0:
  39.8 54.6 all-gather.4
  96.6 37.2 all-gather.2
where the time goes:
time: 147 us
  waiting for transfers between devices  44.3 us (30%)
  starting transfers between devices  40.6 us (28%)
  Pallas kernels  39.1 us (27%)
  between operations  14.3 us (10%)
  local copies, waits for them, and re-layouts  7.16 us (5%)
    ppermute x6, waiting for transfers between devices, rotate(): lax.ppermute(value, axis, [(i, (i + steps) % count) for i in range(count)])  21.1 us
    ppermute x9, starting transfers between devices, swap(): lax.ppermute(value, axis, [(i, i ^ mask) for i in range(lax.axis_size(axi...  14.7 us
    ppermute x6, starting transfers between devices, rotate(): lax.ppermute(value, axis, [(i, (i + steps) % count) for i in range(count)])  14.1 us
    ppermute x4, waiting for transfers between devices, shift(): return lax.ppermute(value, axis, pairs)  12.6 us
    ppermute x4, starting transfers between devices, shift(): return lax.ppermute(value, axis, pairs)  11.1 us
    pallas_call x2, Pallas kernels, products(): pl.pallas_call(partial(products_kernel, len(pairs), base is not None), gr...  8.63 us
    pallas_call x2, Pallas kernels, project(): pl.pallas_call(project_kernel, in_specs=[anywhere] * (len(weights) + 1),...  8.54 us
    pallas_call x2, Pallas kernels, weight_terms(): pl.pallas_call(partial(terms_kernel, chips), in_specs=[vmem, vmem, anywhe...  7.5 us
  transfers between devices with their start and end apart: 22, of which 6 were waited for; matrix products, arithmetic and copies ran while one was open for 0% of the time, Pallas kernels for 22%

commit v1 on v0

--- a/solution.py
+++ b/solution.py
@@ -218,14 +218,14 @@
             flops=4 * cols * rows * kept * chips, bytes_accessed=10 * MIB, transcendentals=0
         ),
         name=name,
-    )(turned, other_turned, inputs, other_inputs)
+    )(turned, other_turned, *in_hbm(inputs), other_inputs)
 
 
 def rows_kernel(n_in, *refs):
     in_refs, out_refs = refs[:n_in], refs[n_in:]
     total = in_refs[0][...]
     for in_ref in in_refs[1:]:
-        total = total + in_ref[...].astype(jnp.float32)
+        total += in_ref[...].astype(jnp.float32)
     at = 0
     for out_ref in out_refs:
         cols = slice(at, at + out_ref.shape[1])
@@ -272,6 +272,7 @@
             )
         flops += 2 * rows * cols * out_width
         if isinstance(right, tuple):
+            lefts[-1:] = in_hbm(left)
             gathered, steps, first = right
             piece = gathered.shape[2]
             rights.append(gathered)
@@ -474,13 +475,12 @@
 
     kv_loc = project(inputs, (key_weight, value_weight), "project_kv")
     kv_list = [kv_loc] + [shift(kv_loc, "ctx", distance) for distance in range(1, SPAN + 1)]
-    late_inputs, kv_loc = lax.optimization_barrier((inputs, kv_loc))
+    other_inputs = swap(inputs, "ctx", 1)
+    late_inputs, other_inputs, kv_loc = lax.optimization_barrier((inputs, other_inputs, kv_loc))
     query = project(late_inputs, (query_weight,), "project_query")
-    query, kv_list, pieces, inputs = lax.optimization_barrier((query, kv_list, pieces, inputs))
+    query, kv_list, pieces = lax.optimization_barrier((query, kv_list, pieces))
     gathered = lax.all_gather(jnp.concatenate(pieces, axis=0), "ctx", axis=0, tiled=True)
     gathered = gathered.reshape(n_ctx, n_head - 1, piece, q_cols + 2 * k_cols)
-
-    other_inputs = swap(inputs, "ctx", 1)
 
     granules = tok_rows // GRAIN
     window_start = (ctx - SPAN) * tok_rows
@@ -501,20 +501,22 @@
     )
     kv_shape = (tok_rows, 2 * k_cols)
     merged, = small_kernel(merge_kernel, [(kv_shape, jnp.bfloat16)], "merge", mid_grads, other_bundle)
+    merged, late_bundle = lax.optimization_barrier((merged, other_bundle))
     merged = shift(merged, "ctx", -2)
 
-    q_terms = weight_terms(bundle, other_bundle, q_cols, inputs, other_inputs, n_ctx, "query_terms")
+    q_terms = weight_terms(bundle, late_bundle, q_cols, inputs, other_inputs, n_ctx, "query_terms")
     q_moved = [swap(q_terms[chips - 1], "ctx", 2 * (chips - 1))]
-    far, merged, dq_up, dq_down, dq_low, q_moved, q_terms = lax.optimization_barrier(
-        (far, merged, dq_up, dq_down, dq_low, q_moved, q_terms)
+    dq_far = rotate(dq_up, "head", 1)
+    far, merged, dq_up, dq_down, dq_low, q_terms = lax.optimization_barrier(
+        (far, merged, dq_up, dq_down, dq_low, q_terms)
     )
     dkv_low, dkv_turned = small_kernel(
         combine_kernel, [(kv_shape, jnp.bfloat16), (kv_shape[::-1], jnp.bfloat16)], "combine",
         own_grads, merged, far, other_bundle,
     )
     dkv_all = lax.all_gather(dkv_low, "head", axis=0, tiled=True)
-    dq_far = rotate(dq_up, "head", 1)
     other_dkv = swap(dkv_turned, "ctx", 1)
+    other_dkv, q_moved = lax.optimization_barrier((other_dkv, q_moved))
     q_moved += [swap(q_terms[chip], "ctx", 2 * chip) for chip in range(1, chips - 1)]
     kv_terms = weight_terms(
         dkv_turned, other_dkv, 2 * k_cols, inputs, other_inputs, n_ctx, "key_terms"

time: 147 us -> 138 us (0.939)
  waiting for transfers between devices: 44.3 us -> 36.8 us
    ppermute x4, waiting for transfers between devices: 12.6 us -> 0.01 us  [shift(): return lax.ppermute(value, axis, pairs)]
    ppermute x9, waiting for transfers between devices: 7.14 us -> 15.4 us  [swap(): lax.ppermute(value, axis, [(i, i ^ mask) for i in range(lax.axis_size(axi...]
    all_gather x1, waiting for transfers between devices: 3.46 us -> 0.01 us  [body(): dkv_all = lax.all_gather(dkv_low, 'head', axis=0, tiled=True)]
    pallas_call x1, Pallas kernels: 7.08 us -> 5.51 us  [attention(): pl.pallas_call(attention_kernel, out_shape=(low, low, bundle, own, sent,...]
    unnamed x34 -> x32, local copies, waits for them, and re-layouts: 7.16 us -> 7.75 us
  transfers between devices with their start and end apart: 22 -> 22, of which waited for: 6 -> 7; matrix products, arithmetic and copies ran while one was open for 0% -> 0% of each run, Pallas kernels for 22% -> 22%
where the time goes in v1:
time: 138 us; the launch traced here: 139 us
  starting transfers between devices  40.7 us (29%)
  Pallas kernels  37.9 us (27%)
  waiting for transfers between devices  36.8 us (27%)
  between operations  14.3 us (10%)
  local copies, waits for them, and re-layouts  7.75 us (6%)
    ppermute x6, waiting for transfers between devices, rotate(): lax.ppermute(value, axis, [(i, (i + steps) % count) for i in range(count)])  21.4 us
    ppermute x9, waiting for transfers between devices, swap(): lax.ppermute(value, axis, [(i, i ^ mask) for i in range(lax.axis_size(axi...  15.4 us
    ppermute x6, starting transfers between devices, rotate(): lax.ppermute(value, axis, [(i, (i + steps) % count) for i in range(count)])  14.7 us
    ppermute x9, starting transfers between devices, swap(): lax.ppermute(value, axis, [(i, i ^ mask) for i in range(lax.axis_size(axi...  14.1 us
    ppermute x4, starting transfers between devices, shift(): return lax.ppermute(value, axis, pairs)  11.1 us
    pallas_call x2, Pallas kernels, products(): pl.pallas_call(partial(products_kernel, len(pairs), base is not None), gr...  9.21 us
    pallas_call x2, Pallas kernels, project(): pl.pallas_call(project_kernel, in_specs=[anywhere] * (len(weights) + 1),...  8.54 us
    unnamed x32, local copies, waits for them, and re-layouts  7.75 us
  transfers between devices with their start and end apart: 22, of which 7 were waited for; matrix products, arithmetic and copies ran while one was open for 0% of the time, Pallas kernels for 22%

profile of v1, /device:TPU:0, one launch (start us, length us, event | category | flops | bytes accessed | tf_op | source)
XLA Modules:
  0.0 138.7 jit_solution(844814002027715758)
XLA Ops:
  7.2 2.0 %cut_rows.1 = (bf16[128,768]{1,0:T(8,128)(2,1)}, bf16[128,768]{1,0:T(8,128)(2,1)}, bf16[128,768]{1,0:T(8,128)(2,1)}) custom-call(bf16[4096,512]{1,0:T(8,128)(2,1)} %refs_3_.1, bf16[4096,128]{1,0:T(8,128)(2,1)} %refs_7_.1, bf16[4096,128]{1,0:T(8,128)(2,1)} %refs_8_.1), custom_call_target="tpu_custom_call" | custom-call | bytes 2097152 | tf_op jit(solution)/shard_map/cut_rows/pallas_call | solution.py:71
  9.8 2.6 %collective-permute-start.4 = (bf16[128,768]{1,0:T(8,128)(2,1)}, bf16[128,768]{1,0:T(8,128)(2,1)S(1)}, u32[]{:S(2)}, u32[]{:S(2)}) collective-permute-start(bf16[128,768]{1,0:T(8,128)(2,1)} %get-tuple-element.71), channel_id=1, source_target_pairs={{0,1},{1,2},{2,3},{3,0},{4,5},{5,6},{6,7},{7,4},{8,9},{9,10},{10,1... | collective-permute-start | bytes 589832 | tf_op jit(solution)/shard_map/ppermute | solution.py:456
  12.4 4.2 %project_kv.1.kv0 = bf16[512,256]{1,0:T(8,128)(2,1)S(1)} custom-call(bf16[512,4096]{1,0:T(8,128)(2,1)} %x_ref.3, bf16[4096,128]{1,0:T(8,128)(2,1)} %refs_7_.1, bf16[4096,128]{1,0:T(8,128)(2,1)} %refs_8_.1), custom_call_target="tpu_custom_call" | custom-call | flops 1073741824 | bytes 6291456 | tf_op jit(solution)/shard_map/project_kv/pallas_call | solution.py:114
  16.7 2.2 %collective-permute-start.1 = (bf16[512,256]{1,0:T(8,128)(2,1)S(1)}, bf16[512,256]{1,0:T(8,128)(2,1)S(1)}, u32[]{:S(2)}, u32[]{:S(2)}) collective-permute-start(bf16[512,256]{1,0:T(8,128)(2,1)S(1)} %project_kv.1.kv0), channel_id=1, source_target_pairs={{0,4},{4,8},{8,12},{12,16},{16,20},{20,24},{24,28},{1,5},{5,9},{9,... | collective-permute-start | bytes 786440 | tf_op jit(solution)/shard_map/ppermute | solution.py:447
  18.9 3.4 %collective-permute-start.2 = (bf16[512,256]{1,0:T(8,128)(2,1)S(1)}, bf16[512,256]{1,0:T(8,128)(2,1)S(1)}, u32[]{:S(2)}, u32[]{:S(2)}) collective-permute-start(bf16[512,256]{1,0:T(8,128)(2,1)S(1)} %project_kv.1.kv0), channel_id=1, source_target_pairs={{0,8},{4,12},{8,16},{12,20},{16,24},{20,28},{1,9},{5,13},{9,17},{1... | collective-permute-start | bytes 786440 | tf_op jit(solution)/shard_map/ppermute | solution.py:447
  22.3 4.2 %collective-permute-start.3 = (bf16[512,256]{1,0:T(8,128)(2,1)S(1)}, bf16[512,256]{1,0:T(8,128)(2,1)S(1)}, u32[]{:S(2)}, u32[]{:S(2)}) collective-permute-start(bf16[512,256]{1,0:T(8,128)(2,1)S(1)} %project_kv.1.kv0), channel_id=1, source_target_pairs={{0,12},{4,16},{8,20},{12,24},{16,28},{1,13},{5,17},{9,21},{13,25},... | collective-permute-start | bytes 786440 | tf_op jit(solution)/shard_map/ppermute | solution.py:447
  26.5 2.0 %copy-done = bf16[512,4096]{1,0:T(8,128)(2,1)} copy-done((bf16[512,4096]{1,0:T(8,128)(2,1)}, bf16[512,4096]{1,0:T(8,128)(2,1)S(1)}, u32[]{:S(2)}) %copy-start) | copy-done | bytes 4194328
  28.5 2.6 %collective-permute-start.5 = (bf16[128,768]{1,0:T(8,128)(2,1)S(1)}, bf16[128,768]{1,0:T(8,128)(2,1)S(1)}, u32[]{:S(2)}, u32[]{:S(2)}) collective-permute-start(bf16[128,768]{1,0:T(8,128)(2,1)S(1)} %copy-done.15), channel_id=1, source_target_pairs={{0,2},{1,3},{2,0},{3,1},{4,6},{5,7},{6,4},{7,5},{8,10},{9,11},{10,... | collective-permute-start | bytes 589832 | tf_op jit(solution)/shard_map/ppermute | solution.py:456
  31.1 1.3 collective-permute-start.6
  32.5 4.3 %project_query.1.query_ref = bf16[512,512]{1,0:T(8,128)(2,1)S(1)} custom-call(bf16[512,4096]{1,0:T(8,128)(2,1)} %x_ref.3, bf16[4096,512]{1,0:T(8,128)(2,1)} %refs_3_.1), custom_call_target="tpu_custom_call" | custom-call | flops 2147483648 | bytes 8388608 | tf_op jit(solution)/shard_map/project_query/pallas_call | solution.py:114
  36.8 4.2 %collective-permute-done.5 = bf16[128,768]{1,0:T(8,128)(2,1)S(1)} collective-permute-done((bf16[128,768]{1,0:T(8,128)(2,1)S(1)}, bf16[128,768]{1,0:T(8,128)(2,1)S(1)}, u32[]{:S(2)}, u32[]{:S(2)}) %collective-permute-start.5) | collective-permute-done | bytes 196640 | tf_op jit(solution)/shard_map/ppermute | solution.py:456
  41.0 0.9 pad_maximum_fusion
  42.4 5.5 %attention.1 = (bf16[512,512]{1,0:T(8,128)(2,1)}, bf16[512,512]{1,0:T(8,128)(2,1)S(1)}, bf16[1024,512]{1,0:T(8,128)(2,1)S(1)}, f32[512,256]{1,0:T(8,128)S(1)}, b...) custom-call(s32[4]{0:T(128)S(1)} %broadcast_subtract_fusion.first_ref, ...), custom_call_target="tpu_custom_call" | custom-call | flops 6442450944 | bytes 6291456 | tf_op jit(solution)/shard_map/attention/pallas_call | solution.py:424
  47.9 2.5 %collective-permute-start.10 = (bf16[1024,512]{1,0:T(8,128)(2,1)S(1)}, bf16[1024,512]{1,0:T(8,128)(2,1)S(1)}, u32[]{:S(2)}, u32[]{:S(2)}) collective-permute-start(bf16[1024,512]{1,0:T(8,128)(2,1)S(1)} %get-tuple-element.84.turned_ref), channel_id=1, source_target_pairs={{0,4},{4,0},{8,12},{12,8},{16,20},{20,16},{24,28},{28,24},{1,5},{5... | collective-permute-start | bytes 3145736 | tf_op jit(solution)/shard_map/ppermute | solution.py:451
  50.4 6.4 %collective-permute-start.12 = (bf16[512,512]{1,0:T(8,128)(2,1)S(1)}, bf16[512,512]{1,0:T(8,128)(2,1)S(1)}, u32[]{:S(2)}, u32[]{:S(2)}) collective-permute-start(bf16[512,512]{1,0:T(8,128)(2,1)S(1)} %get-tuple-element.108.refs_0_), channel_id=1, source_target_pairs={{0,3},{1,0},{2,1},{3,2},{4,7},{5,4},{6,5},{7,6},{8,11},{9,8},{10,9... | collective-permute-start | bytes 1572872 | tf_op jit(solution)/shard_map/ppermute | solution.py:456
  57.6 1.3 collective-permute-start.11
  58.9 4.2 %query_terms.1 = (f32[512,512]{1,0:T(8,128)S(1)}, bf16[512,512]{1,0:T(8,128)(2,1)S(1)}, bf16[512,512]{1,0:T(8,128)(2,1)}, bf16[512,512]{1,0:T(8,128)(2,1)S(1)}) custom-call(bf16[1024,512]{1,0:T(8,128)(2,1)S(1)} %get-tuple-element.84.turned_ref, bf16[1024,512]{1,0:T(8,128)(2,1)S(1)} %collective-permute-done.10.bundle_ref.other_turned_ref, ...), custom_call_target="tpu_custom_call" | custom-call | flops 2147483648 | bytes 10485760 | tf_op jit(solution)/shard_map/query_terms/pallas_call | solution.py:201
  63.1 6.0 %collective-permute-done.12.refs_2_ = bf16[512,512]{1,0:T(8,128)(2,1)S(1)} collective-permute-done((bf16[512,512]{1,0:T(8,128)(2,1)S(1)}, bf16[512,512]{1,0:T(8,128)(2,1)S(1)}, u32[]{:S(2)}, u32[]{:S(2)}) %collective-permute-start.12) | collective-permute-done | bytes 524320 | tf_op jit(solution)/shard_map/ppermute | solution.py:456
  69.1 11.1 %collective-permute-done.7.refs_1_ = bf16[512,512]{1,0:T(8,128)(2,1)} collective-permute-done((bf16[512,512]{1,0:T(8,128)(2,1)S(1)}, bf16[512,512]{1,0:T(8,128)(2,1)}, u32[]{:S(2)}, u32[]{:S(2)}) %collective-permute-start.7) | collective-permute-done | bytes 524320 | tf_op jit(solution)/shard_map/ppermute | solution.py:456
  81.1 6.9 %collective-permute-start.14 = (bf16[512,512]{1,0:T(8,128)(2,1)S(1)}, bf16[512,512]{1,0:T(8,128)(2,1)S(1)}, u32[]{:S(2)}, u32[]{:S(2)}) collective-permute-start(bf16[512,512]{1,0:T(8,128)(2,1)S(1)} %get-tuple-element.91), channel_id=1, source_target_pairs={{0,24},{4,28},{8,16},{12,20},{16,8},{20,12},{24,0},{28,4},{1,25},{... | collective-permute-start | bytes 1572872 | tf_op jit(solution)/shard_map/ppermute | solution.py:451
  88.7 1.8 %collective-permute-start.8 = (bf16[512,512]{1,0:T(8,128)(2,1)}, bf16[512,512]{1,0:T(8,128)(2,1)}, u32[]{:S(2)}, u32[]{:S(2)}) collective-permute-start(bf16[512,512]{1,0:T(8,128)(2,1)} %collective-permute-done.7.refs_1_), channel_id=1, source_target_pairs={{0,1},{1,2},{2,3},{3,0},{4,5},{5,6},{6,7},{7,4},{8,9},{9,10},{10,1... | collective-permute-start | bytes 1572872 | tf_op jit(solution)/shard_map/ppermute | solution.py:456
  90.5 10.4 %collective-permute-done.14.refs_1_ = bf16[512,512]{1,0:T(8,128)(2,1)S(1)} collective-permute-done((bf16[512,512]{1,0:T(8,128)(2,1)S(1)}, bf16[512,512]{1,0:T(8,128)(2,1)S(1)}, u32[]{:S(2)}, u32[]{:S(2)}) %collective-permute-start.14) | collective-permute-done | bytes 524320 | tf_op jit(solution)/shard_map/ppermute | solution.py:451
  101.7 2.2 %copy-done.2 = bf16[512,4096]{1,0:T(8,128)(2,1)S(1)} copy-done((bf16[512,4096]{1,0:T(8,128)(2,1)S(1)}, bf16[512,4096]{1,0:T(8,128)(2,1)}, u32[]{:S(2)}) %copy-start.2) | copy-done | bytes 4194328
  103.9 3.2 %key_terms.1 = (f32[256,512]{1,0:T(8,128)S(1)}, bf16[256,512]{1,0:T(8,128)(2,1)}, bf16[256,512]{1,0:T(8,128)(2,1)}, bf16[256,512]{1,0:T(8,128)(2,1)}) custom-call(bf16[256,512]{1,0:T(8,128)(2,1)S(1)} %get-tuple-element.99.turned_ref, bf16[256,512]{1,0:T(8,128)(2,1)S(1)} %collective-permute-done.13.other_turned_ref, bf16[512,4096]{1,0:T(8,128)(2,1)} %x_ref.3, ...), custom_call_target="tpu_custom_call" | custom-call | flops 1073741824 | bytes 10485760 | tf_op jit(solution)/shard_map/key_terms/pallas_call | solution.py:201
  107.9 3.5 %collective-permute-start.18 = (bf16[256,512]{1,0:T(8,128)(2,1)}, bf16[256,512]{1,0:T(8,128)(2,1)}, u32[]{:S(2)}, u32[]{:S(2)}) collective-permute-start(bf16[256,512]{1,0:T(8,128)(2,1)} %get-tuple-element.103), channel_id=1, source_target_pairs={{0,16},{4,20},{8,24},{12,28},{16,0},{20,4},{24,8},{28,12},{1,17},{... | collective-permute-start | bytes 786440 | tf_op jit(solution)/shard_map/ppermute | solution.py:451
  112.6 1.0 copy-done.4
  113.6 4.0 %products_near.1.refs_12_ = f32[512,1024]{1,0:T(8,128)S(1)} custom-call(bf16[512,512]{1,0:T(8,128)(2,1)S(1)} %copy-done.4, bf16[512,512]{1,0:T(8,128)(2,1)} %collective-permute-done.7.refs_1_, bf16[512,512]{1,0:T(8,128)(2,1)} %copy-done.12, bf16[4096,512]{1,0:T(8,128)(2,1)} %refs_3_.1, bf16[8,3,128,768]{3,2,1,0:T(8,128)(2,1)} %bitcast.3, ...), custom_call_target="tpu_custom_call" | custom-call | flops 1610612736 | bytes 8388608 | tf_op jit(solution)/shard_map/products_near/pallas_call | solution.py:292
  117.7 3.6 %collective-permute-done.18.refs_2_ = bf16[256,512]{1,0:T(8,128)(2,1)} collective-permute-done((bf16[256,512]{1,0:T(8,128)(2,1)}, bf16[256,512]{1,0:T(8,128)(2,1)}, u32[]{:S(2)}, u32[]{:S(2)}) %collective-permute-start.18) | collective-permute-done | bytes 262176 | tf_op jit(solution)/shard_map/ppermute | solution.py:451
  121.2 1.1 collective-permute-done.19.refs_3_
  122.3 2.0 %key_rows.1 = (f32[512,128]{1,0:T(8,128)}, f32[512,128]{1,0:T(8,128)}) custom-call(f32[256,512]{1,0:T(8,128)S(1)} %copy-done.10, bf16[256,512]{1,0:T(8,128)(2,1)S(1)} %collective-permute-done.17.refs_1_, bf16[256,512]{1,0:T(8,128)(2,1)} %collective-permute-done.18.refs_2_, bf16[256,512]{1,0:T(8,128)(2,1)} %collective-permute-done.19.refs_3_), custom_call_target="tpu_custom_call" | custom-call | flops 4194304 | bytes 4194304 | tf_op jit(solution)/shard_map/key_rows/pallas_call | solution.py:155
  124.3 2.4 %query_rows.1 = f32[512,512]{1,0:T(8,128)} custom-call(f32[512,512]{1,0:T(8,128)S(1)} %get-tuple-element.98.refs_0_, bf16[512,512]{1,0:T(8,128)(2,1)S(1)} %copy-done.6, bf16[512,512]{1,0:T(8,128)(2,1)S(1)} %copy-done.8, bf16[512,512]{1,0:T(8,128)(2,1)} %collective-permute-done.16.refs_3_), custom_call_target="tpu_custom_call" | custom-call | flops 4194304 | bytes 4194304 | tf_op jit(solution)/shard_map/query_rows/pallas_call | solution.py:155
  126.7 5.2 %products_far.1 = bf16[512,1024]{1,0:T(8,128)(2,1)} custom-call(bf16[512,512]{1,0:T(8,128)(2,1)} %collective-permute-done.8.refs_0_, bf16[512,256]{1,0:T(8,128)(2,1)} %get-tuple-element.94.refs_1_.refs_2_, bf16[512,256]{1,0:T(8,128)(2,1)} %get-tuple-element.94.refs_1_.refs_2_, bf16[2048,256]{1,0:T(8,128)(2,1)} %all-gather.3.cloned.1.call-done.refs_3_.refs_4_.refs_5_, ...), custom_call_target="tpu_custom_call" | custom-call | flops 1610612736 | bytes 8388608 | tf_op jit(solution)/shard_map/products_far/pallas_call | solution.py:292
  (63 shorter events, 6.1 us)
Async XLA Ops:
  7.2 105.4 %all-gather.5.cloned.1.call-start = ((), (), s32[]{:S(2)}) async-start(), calls=%async_computation.1 | async-start | bytes 5308416 | tf_op jit(solution)/shard_map/all_gather | solution.py:482
  9.2 19.3 %copy-start.15 = (bf16[128,768]{1,0:T(8,128)(2,1)S(1)}, bf16[128,768]{1,0:T(8,128)(2,1)}, u32[]{:S(2)}) copy-start(bf16[128,768]{1,0:T(8,128)(2,1)} %get-tuple-element.72) | copy-start | bytes 589828
  9.2 21.9 %copy-start.14 = (bf16[128,768]{1,0:T(8,128)(2,1)S(1)}, bf16[128,768]{1,0:T(8,128)(2,1)}, u32[]{:S(2)}) copy-start(bf16[128,768]{1,0:T(8,128)(2,1)} %get-tuple-element.73) | copy-start | bytes 589828
  9.3 17.2 %collective-permute-start = (bf16[512,4096]{1,0:T(8,128)(2,1)}, bf16[512,4096]{1,0:T(8,128)(2,1)S(1)}, u32[]{:S(2)}, u32[]{:S(2)}) collective-permute-start(bf16[512,4096]{1,0:T(8,128)(2,1)} %x_ref.3), channel_id=1, source_target_pairs={{0,4},{4,0},{8,12},{12,8},{16,20},{20,16},{24,28},{28,24},{1,5},{5... | collective-permute-start | bytes 12582920 | tf_op jit(solution)/shard_map/ppermute | solution.py:451
  9.8 21.3 %collective-permute-start.4 = (bf16[128,768]{1,0:T(8,128)(2,1)}, bf16[128,768]{1,0:T(8,128)(2,1)S(1)}, u32[]{:S(2)}, u32[]{:S(2)}) collective-permute-start(bf16[128,768]{1,0:T(8,128)(2,1)} %get-tuple-element.71), channel_id=1, source_target_pairs={{0,1},{1,2},{2,3},{3,0},{4,5},{5,6},{6,7},{7,4},{8,9},{9,10},{10,1... | collective-permute-start | bytes 589832 | tf_op jit(solution)/shard_map/ppermute | solution.py:456
  16.6 25.3 %copy-start.13 = (s32[8]{0:T(128)S(1)}, s32[8]{0:T(128)}, u32[]{:S(2)}) copy-start(s32[8]{0:T(128)} %param.11) | copy-start | bytes 100
  16.7 25.7 %copy-start.11 = (bf16[512,512]{1,0:T(8,128)(2,1)S(1)}, bf16[512,512]{1,0:T(8,128)(2,1)}, u32[]{:S(2)}) copy-start(bf16[512,512]{1,0:T(8,128)(2,1)} %grad_ref.1) | copy-start | bytes 1572868
  16.7 24.3 %collective-permute-start.1 = (bf16[512,256]{1,0:T(8,128)(2,1)S(1)}, bf16[512,256]{1,0:T(8,128)(2,1)S(1)}, u32[]{:S(2)}, u32[]{:S(2)}) collective-permute-start(bf16[512,256]{1,0:T(8,128)(2,1)S(1)} %project_kv.1.kv0), channel_id=1, source_target_pairs={{0,4},{4,8},{8,12},{12,16},{16,20},{20,24},{24,28},{1,5},{5,9},{9,... | collective-permute-start | bytes 786440 | tf_op jit(solution)/shard_map/ppermute | solution.py:447
  18.9 22.1 %collective-permute-start.2 = (bf16[512,256]{1,0:T(8,128)(2,1)S(1)}, bf16[512,256]{1,0:T(8,128)(2,1)S(1)}, u32[]{:S(2)}, u32[]{:S(2)}) collective-permute-start(bf16[512,256]{1,0:T(8,128)(2,1)S(1)} %project_kv.1.kv0), channel_id=1, source_target_pairs={{0,8},{4,12},{8,16},{12,20},{16,24},{20,28},{1,9},{5,13},{9,17},{1... | collective-permute-start | bytes 786440 | tf_op jit(solution)/shard_map/ppermute | solution.py:447
  22.3 18.7 %collective-permute-start.3 = (bf16[512,256]{1,0:T(8,128)(2,1)S(1)}, bf16[512,256]{1,0:T(8,128)(2,1)S(1)}, u32[]{:S(2)}, u32[]{:S(2)}) collective-permute-start(bf16[512,256]{1,0:T(8,128)(2,1)S(1)} %project_kv.1.kv0), channel_id=1, source_target_pairs={{0,12},{4,16},{8,20},{12,24},{16,28},{1,13},{5,17},{9,21},{13,25},... | collective-permute-start | bytes 786440 | tf_op jit(solution)/shard_map/ppermute | solution.py:447
  28.5 12.5 %collective-permute-start.5 = (bf16[128,768]{1,0:T(8,128)(2,1)S(1)}, bf16[128,768]{1,0:T(8,128)(2,1)S(1)}, u32[]{:S(2)}, u32[]{:S(2)}) collective-permute-start(bf16[128,768]{1,0:T(8,128)(2,1)S(1)} %copy-done.15), channel_id=1, source_target_pairs={{0,2},{1,3},{2,0},{3,1},{4,6},{5,7},{6,4},{7,5},{8,10},{9,11},{10,... | collective-permute-start | bytes 589832 | tf_op jit(solution)/shard_map/ppermute | solution.py:456
  31.1 9.9 %collective-permute-start.6 = (bf16[128,768]{1,0:T(8,128)(2,1)S(1)}, bf16[128,768]{1,0:T(8,128)(2,1)S(1)}, u32[]{:S(2)}, u32[]{:S(2)}) collective-permute-start(bf16[128,768]{1,0:T(8,128)(2,1)S(1)} %copy-done.14), channel_id=1, source_target_pairs={{0,3},{1,0},{2,1},{3,2},{4,7},{5,4},{6,5},{7,6},{8,11},{9,8},{10,9... | collective-permute-start | bytes 589832 | tf_op jit(solution)/shard_map/ppermute | solution.py:456
  41.9 84.8 %all-gather.3.cloned.1.call-start = ((), (), s32[]{:S(2)}) async-start(), calls=%async_computation | async-start | bytes 1310720 | tf_op jit(solution)/shard_map/all_gather | solution.py:517
  42.3 16.5 %copy-start.1 = (bf16[512,4096]{1,0:T(8,128)(2,1)S(1)}, bf16[512,4096]{1,0:T(8,128)(2,1)}, u32[]{:S(2)}) copy-start(bf16[512,4096]{1,0:T(8,128)(2,1)} %copy-done) | copy-start | bytes 12582916
  47.9 15.2 %copy-start.3 = (bf16[512,512]{1,0:T(8,128)(2,1)}, bf16[512,512]{1,0:T(8,128)(2,1)S(1)}, u32[]{:S(2)}) copy-start(bf16[512,512]{1,0:T(8,128)(2,1)S(1)} %get-tuple-element.108.refs_0_) | copy-start | bytes 1572868
  47.9 9.6 %collective-permute-start.10 = (bf16[1024,512]{1,0:T(8,128)(2,1)S(1)}, bf16[1024,512]{1,0:T(8,128)(2,1)S(1)}, u32[]{:S(2)}, u32[]{:S(2)}) collective-permute-start(bf16[1024,512]{1,0:T(8,128)(2,1)S(1)} %get-tuple-element.84.turned_ref), channel_id=1, source_target_pairs={{0,4},{4,0},{8,12},{12,8},{16,20},{20,16},{24,28},{28,24},{1,5},{5... | collective-permute-start | bytes 3145736 | tf_op jit(solution)/shard_map/ppermute | solution.py:451
  50.4 18.7 %collective-permute-start.12 = (bf16[512,512]{1,0:T(8,128)(2,1)S(1)}, bf16[512,512]{1,0:T(8,128)(2,1)S(1)}, u32[]{:S(2)}, u32[]{:S(2)}) collective-permute-start(bf16[512,512]{1,0:T(8,128)(2,1)S(1)} %get-tuple-element.108.refs_0_), channel_id=1, source_target_pairs={{0,3},{1,0},{2,1},{3,2},{4,7},{5,4},{6,5},{7,6},{8,11},{9,8},{10,9... | collective-permute-start | bytes 1572872 | tf_op jit(solution)/shard_map/ppermute | solution.py:456
  56.8 23.5 %collective-permute-start.7 = (bf16[512,512]{1,0:T(8,128)(2,1)S(1)}, bf16[512,512]{1,0:T(8,128)(2,1)}, u32[]{:S(2)}, u32[]{:S(2)}) collective-permute-start(bf16[512,512]{1,0:T(8,128)(2,1)S(1)} %get-tuple-element.108.refs_0_), channel_id=1, source_target_pairs={{0,1},{1,2},{2,3},{3,0},{4,5},{5,6},{6,7},{7,4},{8,9},{9,10},{10,1... | collective-permute-start | bytes 1572872 | tf_op jit(solution)/shard_map/ppermute | solution.py:456
  56.8 6.3 %collective-permute-start.9 = (bf16[512,256]{1,0:T(8,128)(2,1)S(1)}, bf16[512,256]{1,0:T(8,128)(2,1)S(1)}, u32[]{:S(2)}, u32[]{:S(2)}) collective-permute-start(bf16[512,256]{1,0:T(8,128)(2,1)S(1)} %get-tuple-element.82), channel_id=1, source_target_pairs={{16,4},{24,12},{17,5},{25,13},{18,6},{26,14},{19,7},{27,15}} | collective-permute-start | bytes 786440 | tf_op jit(solution)/shard_map/ppermute | solution.py:499
  57.6 22.7 %collective-permute-start.11 = (bf16[512,256]{1,0:T(8,128)(2,1)S(1)}, bf16[512,256]{1,0:T(8,128)(2,1)S(1)}, u32[]{:S(2)}, u32[]{:S(2)}) collective-permute-start(bf16[512,256]{1,0:T(8,128)(2,1)S(1)} %merge.1), channel_id=1, source_target_pairs={{8,0},{12,4},{16,8},{20,12},{24,16},{28,20},{9,1},{13,5},{17,9},{2... | collective-permute-start | bytes 786440 | tf_op jit(solution)/shard_map/ppermute | solution.py:447
  69.1 12.0 %copy-start.12 = (bf16[512,512]{1,0:T(8,128)(2,1)}, bf16[512,512]{1,0:T(8,128)(2,1)S(1)}, u32[]{:S(2)}) copy-start(bf16[512,512]{1,0:T(8,128)(2,1)S(1)} %collective-permute-done.12.refs_2_) | copy-start | bytes 1572868
  81.1 19.8 %collective-permute-start.14 = (bf16[512,512]{1,0:T(8,128)(2,1)S(1)}, bf16[512,512]{1,0:T(8,128)(2,1)S(1)}, u32[]{:S(2)}, u32[]{:S(2)}) collective-permute-start(bf16[512,512]{1,0:T(8,128)(2,1)S(1)} %get-tuple-element.91), channel_id=1, source_target_pairs={{0,24},{4,28},{8,16},{12,20},{16,8},{20,12},{24,0},{28,4},{1,25},{... | collective-permute-start | bytes 1572872 | tf_op jit(solution)/shard_map/ppermute | solution.py:451
  88.1 23.6 %collective-permute-start.15 = (bf16[512,512]{1,0:T(8,128)(2,1)S(1)}, bf16[512,512]{1,0:T(8,128)(2,1)S(1)}, u32[]{:S(2)}, u32[]{:S(2)}) collective-permute-start(bf16[512,512]{1,0:T(8,128)(2,1)S(1)} %get-tuple-element.112), channel_id=1, source_target_pairs={{0,8},{4,12},{8,0},{12,4},{16,24},{20,28},{24,16},{28,20},{1,9},{5... | collective-permute-start | bytes 1572872 | tf_op jit(solution)/shard_map/ppermute | solution.py:451
  88.1 13.6 %collective-permute-start.13 = (bf16[256,512]{1,0:T(8,128)(2,1)S(1)}, bf16[256,512]{1,0:T(8,128)(2,1)S(1)}, u32[]{:S(2)}, u32[]{:S(2)}) collective-permute-start(bf16[256,512]{1,0:T(8,128)(2,1)S(1)} %get-tuple-element.99.turned_ref), channel_id=1, source_target_pairs={{0,4},{4,0},{8,12},{12,8},{16,20},{20,16},{24,28},{28,24},{1,5},{5... | collective-permute-start | bytes 786440 | tf_op jit(solution)/shard_map/ppermute | solution.py:451
  88.1 29.6 %collective-permute-start.16 = (bf16[512,512]{1,0:T(8,128)(2,1)}, bf16[512,512]{1,0:T(8,128)(2,1)}, u32[]{:S(2)}, u32[]{:S(2)}) collective-permute-start(bf16[512,512]{1,0:T(8,128)(2,1)} %get-tuple-element.113), channel_id=1, source_target_pairs={{0,16},{4,20},{8,24},{12,28},{16,0},{20,4},{24,8},{28,12},{1,17},{... | collective-permute-start | bytes 1572872 | tf_op jit(solution)/shard_map/ppermute | solution.py:451
  88.7 37.9 %collective-permute-start.8 = (bf16[512,512]{1,0:T(8,128)(2,1)}, bf16[512,512]{1,0:T(8,128)(2,1)}, u32[]{:S(2)}, u32[]{:S(2)}) collective-permute-start(bf16[512,512]{1,0:T(8,128)(2,1)} %collective-permute-done.7.refs_1_), channel_id=1, source_target_pairs={{0,1},{1,2},{2,3},{3,0},{4,5},{5,6},{6,7},{7,4},{8,9},{9,10},{10,1... | collective-permute-start | bytes 1572872 | tf_op jit(solution)/shard_map/ppermute | solution.py:456
  107.9 9.8 %collective-permute-start.17 = (bf16[256,512]{1,0:T(8,128)(2,1)}, bf16[256,512]{1,0:T(8,128)(2,1)S(1)}, u32[]{:S(2)}, u32[]{:S(2)}) collective-permute-start(bf16[256,512]{1,0:T(8,128)(2,1)} %get-tuple-element.102), channel_id=1, source_target_pairs={{0,8},{4,12},{8,0},{12,4},{16,24},{20,28},{24,16},{28,20},{1,9},{5... | collective-permute-start | bytes 786440 | tf_op jit(solution)/shard_map/ppermute | solution.py:451
  107.9 13.3 %collective-permute-start.18 = (bf16[256,512]{1,0:T(8,128)(2,1)}, bf16[256,512]{1,0:T(8,128)(2,1)}, u32[]{:S(2)}, u32[]{:S(2)}) collective-permute-start(bf16[256,512]{1,0:T(8,128)(2,1)} %get-tuple-element.103), channel_id=1, source_target_pairs={{0,16},{4,20},{8,24},{12,28},{16,0},{20,4},{24,8},{28,12},{1,17},{... | collective-permute-start | bytes 786440 | tf_op jit(solution)/shard_map/ppermute | solution.py:451
  112.6 9.8 %collective-permute-start.19 = (bf16[256,512]{1,0:T(8,128)(2,1)}, bf16[256,512]{1,0:T(8,128)(2,1)}, u32[]{:S(2)}, u32[]{:S(2)}) collective-permute-start(bf16[256,512]{1,0:T(8,128)(2,1)} %get-tuple-element.104), channel_id=1, source_target_pairs={{0,24},{4,28},{8,16},{12,20},{16,8},{20,12},{24,0},{28,4},{1,25},{... | collective-permute-start | bytes 786440 | tf_op jit(solution)/shard_map/ppermute | solution.py:451
  113.6 8.7 %copy-start.10 = (f32[256,512]{1,0:T(8,128)S(1)}, f32[256,512]{1,0:T(8,128)}, u32[]{:S(2)}) copy-start(f32[256,512]{1,0:T(8,128)} %copy-done.9) | copy-start | bytes 1572868
  113.6 10.7 %copy-start.6 = (bf16[512,512]{1,0:T(8,128)(2,1)S(1)}, bf16[512,512]{1,0:T(8,128)(2,1)}, u32[]{:S(2)}) copy-start(bf16[512,512]{1,0:T(8,128)(2,1)} %copy-done.5) | copy-start | bytes 1572868
  113.6 10.7 %copy-start.8 = (bf16[512,512]{1,0:T(8,128)(2,1)S(1)}, bf16[512,512]{1,0:T(8,128)(2,1)}, u32[]{:S(2)}) copy-start(bf16[512,512]{1,0:T(8,128)(2,1)} %copy-done.7) | copy-start | bytes 1572868
  (6 other events, 7.7 us)
Sparse Core Ops, SparseCore 0:
  42.0 49.4 all-gather.4
  93.0 28.9 all-gather.2
